TPU v7x, 256 devices: a whole 4x4x8 slice. The times are simulated.
256 devices in a mesh: gx: 16 (over y_lo, x, core), gy: 8 (over z), ga: 2 (over y_hi).
Axes of the slice: x: 4, y: 4 (y_hi: 2, y_lo: 2; y = y_hi * 2 + y_lo), z: 8, core: 2. Of those that a mesh axis runs over, the one named last changes fastest.
Arguments:
- field: float32 [64, 512, 1024], P('ga', 'gx', 'gy'), may hold values from -25 to 25
- prev_field: float32 [64, 512, 1024], P('ga', 'gx', 'gy'), may hold values from -25 to 25
- diffusivity: float32 [64, 512, 1024], P('ga', 'gx', 'gy'), may hold values from 0.03 to 0.1
- velocity: float32 [3, 64, 512, 1024], P(None, 'ga', 'gx', 'gy'), may hold values from -0.13 to 0.13
- w_lift: bfloat16 [27, 128], replicated, may hold values from -1.25 to 1.25
- norm_gain: float32 [128], replicated, may hold values from 0.1 to 1.9
- w_conv: bfloat16 [16, 3456, 128], P('gx'), may hold values from -0.109375 to 0.109375
- w_out: bfloat16 [128], replicated, may hold values from -0.5 to 0.5
- tile_count: int32 [2, 16, 8], P('ga', 'gx', 'gy'), may hold values from 1 to 2, as said below
- patch_dest: int32 [2, 16, 8, 2], P('ga', 'gx', 'gy'), may hold values from 0 to 15, as said below
- anchor_x: int32 [2, 16, 8, 2], P('ga', 'gx', 'gy'), may hold values from 0 to 24
- anchor_y: int32 [2, 16, 8, 2], P('ga', 'gx', 'gy'), may hold values from 0 to 124
Outputs:
- new_field: float32 [64, 512, 1024], P('ga', 'gx', 'gy')
- learner_loss: float32 [2, 16, 8], P('ga', 'gx', 'gy')
- dir_lift: float32 [27, 128], replicated
- dir_gain: float32 [128], replicated
- dir_conv: float32 [16, 3456, 128], P('gx')
- dir_out: float32 [128], replicated
Inputs may be any that keep to these rules, and one draw needn't show every extreme that they name: `tile_count`: in every line of tiles along x, at least two tiles yield 2 patches. `patch_dest`: among the valid slots of one line of tiles along x, at most 4 go to one learner, and in every line exactly 4 go to some learner; slots beyond a tile's count carry no patch.
All inputs are finite; a program needn't handle non-finite values.
Results may differ from a plain program's by a relative error of at most 0.004.
Values may be sent and summed in bfloat16 or wider, within the bound.
A program may use at most 128 MiB of HBM per device.

v0:
```python
import jax
import jax.numpy as jnp
from jax import lax
from jax.sharding import PartitionSpec as P

PX = 8
PY = 4
STEPS = 2
PVOX = 1024


def padded_2(cells, sides, width, closed):
    for axis, dim in sides:
        count = lax.axis_size(axis)
        ends = count if closed else count - 1
        head = lax.slice_in_dim(cells, 0, width, axis=dim)
        tail = lax.slice_in_dim(cells, cells.shape[dim] - width, cells.shape[dim], axis=dim)
        cells = jnp.concatenate(
            [
                lax.ppermute(tail, axis, [(i, (i + 1) % count) for i in range(ends)]),
                cells,
                lax.ppermute(head, axis, [((i + 1) % count, i) for i in range(ends)]),
            ],
            axis=dim,
        )
    return cells


def neighbours(volume):
    extent_z, extent_x, extent_y = (volume.shape[0], volume.shape[1], volume.shape[2])
    padded = jnp.pad(volume, ((1, 1), (1, 1), (1, 1), (0, 0)))
    pieces = []
    for shift_z in range(3):
        for shift_x in range(3):
            for shift_y in range(3):
                pieces.append(
                    padded[
                        shift_z : shift_z + extent_z,
                        shift_x : shift_x + extent_x,
                        shift_y : shift_y + extent_y,
                        :,
                    ]
                )
    return jnp.concatenate(pieces, axis=3).reshape(extent_z * extent_x * extent_y, -1)


def surrogate(params, inputs):
    w_lift, norm_gain, w_conv, w_out = params
    extent_z, extent_x, extent_y = inputs.shape
    lifted = jax.nn.gelu(
        jnp.dot(neighbours(inputs[..., None]), w_lift, preferred_element_type=jnp.float32)
    ).astype(jnp.bfloat16)
    widened = lax.optimization_barrier(lifted).astype(jnp.float32)
    normed = (
        widened * lax.rsqrt(jnp.mean(widened * widened, axis=1, keepdims=True) + 1e-06) * norm_gain
    ).astype(jnp.bfloat16)
    mixed = jax.nn.gelu(
        jnp.dot(
            neighbours(normed.reshape(extent_z, extent_x, extent_y, -1)),
            w_conv,
            preferred_element_type=jnp.float32,
        )
    )
    hidden = (widened + mixed).astype(jnp.bfloat16)
    return jnp.dot(hidden, w_out, preferred_element_type=jnp.float32)


def patch_terms(params, inputs, target, weight):

    def loss_of(params):
        prediction = surrogate(params, inputs)
        misfit = prediction - target.reshape(-1).astype(jnp.float32)
        return weight * 0.5 * jnp.sum(misfit * misfit)

    patch_loss, pullback = jax.vjp(loss_of, params)
    return (patch_loss, pullback(jnp.ones((), jnp.float32))[0])


def advance(extended, diffusivity, velocity):
    centre = extended[1:-1, 1:-1, 1:-1]
    below = extended[:-2, 1:-1, 1:-1]
    above = extended[2:, 1:-1, 1:-1]
    behind = extended[1:-1, :-2, 1:-1]
    ahead = extended[1:-1, 2:, 1:-1]
    left_side = extended[1:-1, 1:-1, :-2]
    right_side = extended[1:-1, 1:-1, 2:]
    laplace = above + below + (ahead + behind) + (right_side + left_side) - 6.0 * centre
    transport = jnp.maximum(velocity[0], 0.0) * (centre - below) + jnp.minimum(velocity[0], 0.0) * (
        above - centre
    )
    transport = transport + (
        jnp.maximum(velocity[1], 0.0) * (centre - behind)
        + jnp.minimum(velocity[1], 0.0) * (ahead - centre)
    )
    transport = transport + (
        jnp.maximum(velocity[2], 0.0) * (centre - left_side)
        + jnp.minimum(velocity[2], 0.0) * (right_side - centre)
    )
    return centre + diffusivity * laplace - transport


def train_slots(params, batch, weights):
    half_width = batch.shape[1] // 2
    layers = half_width // (PX * PY)

    def slot_step(running, slot_item):
        record, weight = slot_item
        inputs = record[:half_width].reshape(layers, PX, PY)
        target = record[half_width:].reshape(layers, PX, PY)
        patch_loss, gradients = patch_terms(params, inputs, target, weight)
        running = jax.tree.map(
            lambda summed, gradient: summed + gradient.astype(jnp.float32), running, gradients
        )
        return (running, patch_loss)

    initial = jax.tree.map(lambda weight: jnp.zeros(weight.shape, jnp.float32), params)
    return lax.scan(slot_step, initial, (batch, weights))


def body(
    field,
    prev_field,
    diffusivity,
    velocity,
    w_lift,
    norm_gain,
    w_conv,
    w_out,
    tile_count,
    patch_dest,
    anchor_x,
    anchor_y,
):
    state = field
    for repeat in range(STEPS):
        layered = padded_2(state, (("ga", 0),), 1, False)
        extended = padded_2(layered, (("gx", 1), ("gy", 2)), 1, True)
        state = advance(extended, diffusivity, velocity)
    slot_count = patch_dest.shape[3]
    layers = field.shape[0]
    count_here = tile_count.reshape(1)
    dest_here = patch_dest.reshape(slot_count)
    start_x = anchor_x.reshape(slot_count)
    start_y = anchor_y.reshape(slot_count)
    pieces = []
    for slot_index in range(slot_count):
        corner = (jnp.int32(0), start_x[slot_index], start_y[slot_index])
        source = lax.dynamic_slice(prev_field, corner, (layers, PX, PY)).reshape(-1)
        wanted = lax.dynamic_slice(field, corner, (layers, PX, PY)).reshape(-1)
        pieces.append(jnp.concatenate([source, wanted]))
    slots_here = jnp.stack(pieces).astype(jnp.bfloat16)
    counts_line, dests_flat = (
        lax.all_gather(count_here, "gx", axis=0, tiled=True),
        lax.all_gather(dest_here, "gx", axis=0, tiled=True),
    )
    learners = lax.axis_size("gx")
    myself = lax.axis_index("gx")
    slot_ids = jnp.arange(slot_count, dtype=jnp.int32)
    device_ids = jnp.arange(learners, dtype=jnp.int32)
    valid_line = slot_ids[None, :] < counts_line[:, None]
    dest_line = dests_flat.reshape(learners, slot_count)
    to_myself = valid_line & (dest_line == myself)
    mine_count = jnp.sum(to_myself.astype(jnp.int32))
    valid_here = slot_ids < count_here[0]
    member_conv = w_conv[0]
    params = (w_lift, norm_gain, member_conv, w_out)
    earlier = slot_ids[None, :] < slot_ids[:, None]
    same_dest = (
        (dest_line[:, :, None] == dest_line[:, None, :]) & valid_line[:, None, :] & earlier[None]
    )
    rank_line = jnp.sum(same_dest.astype(jnp.int32), axis=2)
    rank_here = lax.dynamic_index_in_dim(rank_line, myself, 0, keepdims=False)
    pick = (
        (dest_here[None, None, :] == device_ids[:, None, None])
        & (rank_here[None, None, :] == slot_ids[None, :, None])
        & valid_here[None, None, :]
    )
    outgoing = jnp.einsum(
        "drk,kv->drv", pick.astype(jnp.bfloat16), slots_here, preferred_element_type=jnp.float32
    ).astype(jnp.bfloat16)
    incoming = lax.all_to_all(outgoing, "gx", split_axis=0, concat_axis=0, tiled=True)
    flat_mine = to_myself.reshape(-1).astype(jnp.int32)
    position = (jnp.cumsum(flat_mine) - flat_mine).reshape(learners, slot_count)
    capacity = 2 * slot_count
    cap_ids = jnp.arange(capacity, dtype=jnp.int32)
    hits = (
        to_myself[None, :, :, None]
        & (position[None, :, :, None] == cap_ids[:, None, None, None])
        & (rank_line[None, :, :, None] == slot_ids[None, None, None, :])
    )
    place = jnp.sum(hits.astype(jnp.float32), axis=2).astype(jnp.bfloat16)
    batch = jnp.einsum("csr,srv->cv", place, incoming, preferred_element_type=jnp.float32).astype(
        jnp.bfloat16
    )
    weights = (cap_ids < mine_count).astype(jnp.float32)
    gradients, losses = train_slots(params, batch, weights)
    loss_sum = jnp.sum(losses)
    learner_loss = (loss_sum / (PVOX * jnp.maximum(mine_count, 1).astype(jnp.float32))).reshape(
        1, 1, 1
    )
    grad_lift, grad_gain, grad_conv, grad_out = gradients
    group_count = lax.axis_size("gy") * lax.axis_size("ga")
    param_count = w_lift.size + norm_gain.size + w_out.size + learners * member_conv.size
    conv_total = lax.psum(grad_conv, ("gy", "ga"))
    conv_squares = jnp.sum(conv_total * conv_total) / group_count
    sum_lift, sum_gain, sum_out, all_squares = lax.psum(
        (grad_lift, grad_gain, grad_out, conv_squares), ("gx", "gy", "ga")
    )
    squares = (
        jnp.sum(sum_lift * sum_lift)
        + jnp.sum(sum_gain * sum_gain)
        + all_squares
        + jnp.sum(sum_out * sum_out)
    )
    scale = lax.rsqrt(squares / param_count + 1e-06)
    dir_conv = (conv_total * scale).reshape(w_conv.shape)
    dir_lift = sum_lift * scale
    dir_gain = sum_gain * scale
    dir_out = sum_out * scale
    return (state, learner_loss, dir_lift, dir_gain, dir_conv, dir_out)


def solution(mesh):
    in_specs = (
        P("ga", "gx", "gy"),
        P("ga", "gx", "gy"),
        P("ga", "gx", "gy"),
        P(None, "ga", "gx", "gy"),
        P(),
        P(),
        P("gx", None, None),
        P(),
        P("ga", "gx", "gy"),
        P("ga", "gx", "gy", None),
        P("ga", "gx", "gy", None),
        P("ga", "gx", "gy", None),
    )
    out_specs = (P("ga", "gx", "gy"), P("ga", "gx", "gy"), P(), P(), P("gx", None, None), P())
    return jax.shard_map(body, mesh=mesh, in_specs=in_specs, out_specs=out_specs, check_vma=False)
```

profile of v0, /device:TPU:1, one launch (start us, length us, event | category | flops | bytes accessed | tf_op | source)
XLA Modules:
  0.0 553.0 jit_solution(15087117499703280097)
XLA Ops:
  24.5 10.8 %all-reduce.31 = (s32[16]{0:T(128)S(1)}, s32[32]{0:T(128)S(1)}) all-reduce(s32[16]{0:T(128)S(1)} %bitcast_dynamic-update-slice_fusion, s32[32]{0:T(128)S(1)} %bitcast_dynamic-update-slice_fusion.1), channel_id=2, replica_groups=mesh['gx'=16,'gy'=8,'ga'=2] {'gx'}, use_global_device_ids=true, to_apply=%add.29 | all-reduce | flops 48 | bytes 384
  37.8 6.5 %all-to-all-start = ((bf16[16,2,2048]{2,1,0:T(2,128)(2,1)}), bf16[16,2,2048]{2,1,0:T(2,128)(2,1)S(1)}, u32[]{:S(2)}, u32[]{:S(2)}) async-start(bf16[16,2,2048]{2,1,0:T(2,128)(2,1)} %copy.99), calls=%async_computation | async-start | bytes 262144 | tf_op jit(solution)/shard_map/all_to_all | solution.py:181
  45.1 4.4 collective-permute-start.1
  61.8 228.4 %while.22 = (s32[]{:T(128)}, f32[27,128]{1,0:T(8,128)}, f32[128]{0:T(128)S(1)}, f32[3456,128]{1,0:T(8,128)}, f32[128]{0:T(128)S(1)}, /*index=5*/f32[4]{0:T(128)}...) while((s32[]{:T(128)}, f32[27,128]{1,0:T(8,128)}, ...), condition=%wide.region_9.10_spmd.clone, body=%wide.region_4.9_spmd.clone.sunk | while | flops 2765799424 | bytes 123144792 | solution.py:117
  78.6 6.5 %fusion.187 = f32[3456,128]{1,0:T(8,128)} fusion(bf16[1024,3456]{1,0:T(8,128)(2,1)} %copy-done.5, f32[3456,128]{1,0:T(8,128)} %get-tuple-element.660, pred[]{:T(512)S(6)} %compare.32, f32[1024,128]{1,0:T(8,128)S(1)} %get-tuple-element.606, f32[128]{0:T(128)S(1)} %convert.77, f32[1024]{0:T(1024)S(1)} %get-tuple-element.609), kind=kOutput, calls=%fused_computation.3.clone.1 | convolution fusion | flops 910622720 | bytes 11145729 | tf_op jit(solution)/shard_map/while/body/eval_jaxpr/transpose(jvp())/dot_general | solution.py:58
  85.1 5.1 convolution_convert_fusion.5
  90.2 12.4 %reshape.609 = bf16[32,8,4,3456]{3,2,1,0:T(4,128)(2,1)} reshape(bf16[1024,3456]{1,0:T(8,128)(2,1)} %convolution_convert_fusion.5) | data formatting | bytes 14155776 | tf_op jit(solution)/shard_map/while/body/eval_jaxpr/transpose(jvp())/reshape | solution.py:44
  102.7 4.8 fusion.181
  109.8 3.5 pad_add_fusion.9
  134.8 7.0 %fusion.187 = f32[3456,128]{1,0:T(8,128)} fusion(bf16[1024,3456]{1,0:T(8,128)(2,1)} %copy-done.5, f32[3456,128]{1,0:T(8,128)} %get-tuple-element.660, pred[]{:T(512)S(6)} %compare.32, f32[1024,128]{1,0:T(8,128)S(1)} %get-tuple-element.606, f32[128]{0:T(128)S(1)} %convert.77, f32[1024]{0:T(1024)S(1)} %get-tuple-element.609), kind=kOutput, calls=%fused_computation.3.clone.1 | convolution fusion | flops 910622720 | bytes 11145729 | tf_op jit(solution)/shard_map/while/body/eval_jaxpr/transpose(jvp())/dot_general | solution.py:58
  141.8 5.1 convolution_convert_fusion.5
  146.9 12.4 %reshape.609 = bf16[32,8,4,3456]{3,2,1,0:T(4,128)(2,1)} reshape(bf16[1024,3456]{1,0:T(8,128)(2,1)} %convolution_convert_fusion.5) | data formatting | bytes 14155776 | tf_op jit(solution)/shard_map/while/body/eval_jaxpr/transpose(jvp())/reshape | solution.py:44
  159.3 4.8 fusion.181
  166.4 3.5 pad_add_fusion.9
  192.1 7.0 %fusion.187 = f32[3456,128]{1,0:T(8,128)} fusion(bf16[1024,3456]{1,0:T(8,128)(2,1)} %copy-done.5, f32[3456,128]{1,0:T(8,128)} %get-tuple-element.660, pred[]{:T(512)S(6)} %compare.32, f32[1024,128]{1,0:T(8,128)S(1)} %get-tuple-element.606, f32[128]{0:T(128)S(1)} %convert.77, f32[1024]{0:T(1024)S(1)} %get-tuple-element.609), kind=kOutput, calls=%fused_computation.3.clone.1 | convolution fusion | flops 910622720 | bytes 11145729 | tf_op jit(solution)/shard_map/while/body/eval_jaxpr/transpose(jvp())/dot_general | solution.py:58
  199.1 5.1 convolution_convert_fusion.5
  204.2 12.4 %reshape.609 = bf16[32,8,4,3456]{3,2,1,0:T(4,128)(2,1)} reshape(bf16[1024,3456]{1,0:T(8,128)(2,1)} %convolution_convert_fusion.5) | data formatting | bytes 14155776 | tf_op jit(solution)/shard_map/while/body/eval_jaxpr/transpose(jvp())/reshape | solution.py:44
  216.7 4.8 fusion.181
  223.8 3.5 pad_add_fusion.9
  249.5 7.0 %fusion.187 = f32[3456,128]{1,0:T(8,128)} fusion(bf16[1024,3456]{1,0:T(8,128)(2,1)} %copy-done.5, f32[3456,128]{1,0:T(8,128)} %get-tuple-element.660, pred[]{:T(512)S(6)} %compare.32, f32[1024,128]{1,0:T(8,128)S(1)} %get-tuple-element.606, f32[128]{0:T(128)S(1)} %convert.77, f32[1024]{0:T(1024)S(1)} %get-tuple-element.609), kind=kOutput, calls=%fused_computation.3.clone.1 | convolution fusion | flops 910622720 | bytes 11145729 | tf_op jit(solution)/shard_map/while/body/eval_jaxpr/transpose(jvp())/dot_general | solution.py:58
  256.5 5.1 convolution_convert_fusion.5
  261.6 12.4 %reshape.609 = bf16[32,8,4,3456]{3,2,1,0:T(4,128)(2,1)} reshape(bf16[1024,3456]{1,0:T(8,128)(2,1)} %convolution_convert_fusion.5) | data formatting | bytes 14155776 | tf_op jit(solution)/shard_map/while/body/eval_jaxpr/transpose(jvp())/reshape | solution.py:44
  274.0 4.8 fusion.181
  281.2 3.5 pad_add_fusion.9
  292.7 5.6 %collective-permute-start.4 = (f32[34,34,1]{1,2,0:T(1,128)S(1)}, f32[34,34,1]{1,2,0:T(1,128)S(1)}, u32[]{:S(2)}, u32[]{:S(2)}) collective-permute-start(f32[34,34,1]{1,2,0:T(1,128)S(1)} %copy.101), channel_id=1, source_target_pairs={{2,0},{4,2},{6,4},{8,6},{10,8},{12,10},{14,12},{0,14},{3,1},{5,3},... | collective-permute-start | bytes 13880 | tf_op jit(solution)/shard_map/ppermute | solution.py:22
  299.6 3.0 collective-permute-done.5
  303.8 3.0 fusion.88
  308.1 5.5 collective-permute-start.7
  314.8 6.5 %collective-permute-start.8 = (f32[34,1,128]{2,1,0:T(1,128)S(1)}, f32[34,1,128]{2,1,0:T(1,128)S(1)}, u32[]{:S(2)}, u32[]{:S(2)}) collective-permute-start(f32[34,1,128]{2,1,0:T(1,128)S(1)} %get-tuple-element.368), channel_id=1, source_target_pairs={{16,0},{32,16},{48,32},{64,48},{80,64},{96,80},{112,96},{128,112},... | collective-permute-start | bytes 52232 | tf_op jit(solution)/shard_map/ppermute | solution.py:22
  331.1 3.0 fusion.68
  336.0 113.2 %all-reduce.35.cloned.1.call-done = f32[3456,128]{1,0:T(8,128)} async-done(((f32[3456,128]{1,0:T(8,128)}), f32[3456,128]{1,0:T(8,128)}) %all-reduce.35.cloned.1.call-update) | async-done | bytes 1769488 | tf_op jit(solution)/shard_map/psum | solution.py:204
  452.3 84.4 %all-reduce.32 = (f32[27,128]{1,0:T(8,128)S(1)}, f32[128]{0:T(128)S(1)}, f32[]{:T(128)}, f32[128]{0:T(128)S(1)}) all-reduce(f32[27,128]{1,0:T(8,128)} %get-tuple-element.193, f32[128]{0:T(128)S(1)} %get-tuple-element.194, f32[]{:T(128)S(6)} %div.26, ...), channel_id=1, replica_groups=mesh['gx'=16,'gy'=8,'ga'=2] {'gx','gy','ga'}, use_global_device_ids=true, to_apply=%region_11.12 | all-reduce | flops 3713 | bytes 29704 | tf_op jit(solution)/shard_map/psum | solution.py:206
  (463 shorter events, 140.5 us)
Async XLA Ops:
  37.8 23.7 %all-to-all-start = ((bf16[16,2,2048]{2,1,0:T(2,128)(2,1)}), bf16[16,2,2048]{2,1,0:T(2,128)(2,1)S(1)}, u32[]{:S(2)}, u32[]{:S(2)}) async-start(bf16[16,2,2048]{2,1,0:T(2,128)(2,1)} %copy.99), calls=%async_computation | async-start | bytes 262144 | tf_op jit(solution)/shard_map/all_to_all | solution.py:181
  44.3 404.9 %all-reduce.35.cloned.1.call-start = ((), (), s32[]{:S(2)}) async-start(), calls=%async_computation.1 | async-start | bytes 3538944 | tf_op jit(solution)/shard_map/psum | solution.py:204
  45.1 7.1 %collective-permute-start.1 = (f32[1,32,128]{2,1,0:T(8,128)S(1)}, f32[1,32,128]{2,1,0:T(8,128)S(1)}, u32[]{:S(2)}, u32[]{:S(2)}) collective-permute-start(f32[1,32,128]{2,1,0:T(8,128)S(1)} %get-tuple-element.379), channel_id=1, source_target_pairs={{0,1},{2,3},{4,5},{6,7},{8,9},{10,11},{12,13},{14,15},{16,17},{18,... | collective-permute-start | bytes 49160 | tf_op jit(solution)/shard_map/ppermute | solution.py:20
  49.5 6.0 %collective-permute-start = (f32[1,32,128]{2,1,0:T(8,128)S(1)}, f32[1,32,128]{2,1,0:T(8,128)S(1)}, u32[]{:S(2)}, u32[]{:S(2)}) collective-permute-start(f32[1,32,128]{2,1,0:T(8,128)S(1)} %get-tuple-element.378), channel_id=1, source_target_pairs={{1,0},{3,2},{5,4},{7,6},{9,8},{11,10},{13,12},{15,14},{17,16},{19,... | collective-permute-start | bytes 49160 | tf_op jit(solution)/shard_map/ppermute | solution.py:22
  52.1 3.4 copy-start.11
  55.5 6.2 %copy-start.4 = (f32[34,32,128]{2,1,0:T(8,128)}, f32[34,32,128]{2,1,0:T(8,128)S(1)}, u32[]{:S(2)}) copy-start(f32[34,32,128]{2,1,0:T(8,128)S(1)} %constant_dynamic-update-slice_fusion.27) | copy-start | bytes 1671172
  56.1 4.5 collective-permute-start.2
  57.7 2.9 collective-permute-start.3
  61.8 228.5 %copy-start.2 = (f32[34,34,128]{2,1,0:T(8,128)S(1)}, f32[34,34,128]{2,1,0:T(8,128)}, u32[]{:S(2)}) copy-start(f32[34,34,128]{2,1,0:T(8,128)} %pad_maximum_fusion) | copy-start | bytes 1775620
  68.6 4.6 copy-start.6
  74.3 4.1 copy-start.5
  124.7 4.6 copy-start.6
  130.5 4.1 copy-start.5
  182.1 4.6 copy-start.6
  187.5 2.5 copy-start.14
  187.8 4.1 copy-start.5
  239.4 4.6 copy-start.6
  244.8 2.5 copy-start.14
  245.2 4.1 copy-start.5
  290.2 13.6 %copy-start.1 = (f32[3,32,32,128]{3,2,1,0:T(8,128)S(1)}, f32[3,32,32,128]{3,2,1,0:T(8,128)}, u32[]{:S(2)}) copy-start(f32[3,32,32,128]{3,2,1,0:T(8,128)} %param.17) | copy-start | bytes 4718596
  290.2 13.6 %copy-start.3 = (f32[32,32,128]{2,1,0:T(8,128)S(1)}, f32[32,32,128]{2,1,0:T(8,128)}, u32[]{:S(2)}) copy-start(f32[32,32,128]{2,1,0:T(8,128)} %param.14) | copy-start | bytes 1572868
  290.2 13.6 %copy-start.8 = (f32[34,1,128]{2,1,0:T(1,128)S(1)}, f32[34,1,128]{2,1,0:T(1,128)}, u32[]{:S(2)}) copy-start(f32[34,1,128]{2,1,0:T(1,128)} %copy-done.7) | copy-start | bytes 52228
  290.2 13.6 %copy-start.10 = (f32[34,1,128]{2,1,0:T(1,128)S(1)}, f32[34,1,128]{2,1,0:T(1,128)}, u32[]{:S(2)}) copy-start(f32[34,1,128]{2,1,0:T(1,128)} %copy-done.9) | copy-start | bytes 52228
  290.2 13.6 %copy-start.12 = (f32[1,32,128]{2,1,0:T(8,128)S(1)}, f32[1,32,128]{2,1,0:T(8,128)}, u32[]{:S(2)}) copy-start(f32[1,32,128]{2,1,0:T(8,128)} %copy-done.11) | copy-start | bytes 49156
  292.7 6.5 %collective-permute-start.4 = (f32[34,34,1]{1,2,0:T(1,128)S(1)}, f32[34,34,1]{1,2,0:T(1,128)S(1)}, u32[]{:S(2)}, u32[]{:S(2)}) collective-permute-start(f32[34,34,1]{1,2,0:T(1,128)S(1)} %copy.101), channel_id=1, source_target_pairs={{2,0},{4,2},{6,4},{8,6},{10,8},{12,10},{14,12},{0,14},{3,1},{5,3},... | collective-permute-start | bytes 13880 | tf_op jit(solution)/shard_map/ppermute | solution.py:22
  298.7 3.9 collective-permute-start.5
  306.8 6.8 %collective-permute-start.6 = (f32[1,32,128]{2,1,0:T(8,128)S(1)}, f32[1,32,128]{2,1,0:T(8,128)S(1)}, u32[]{:S(2)}, u32[]{:S(2)}) collective-permute-start(f32[1,32,128]{2,1,0:T(8,128)S(1)} %get-tuple-element.377), channel_id=1, source_target_pairs={{1,0},{3,2},{5,4},{7,6},{9,8},{11,10},{13,12},{15,14},{17,16},{19,... | collective-permute-start | bytes 49160 | tf_op jit(solution)/shard_map/ppermute | solution.py:22
  308.1 6.7 %collective-permute-start.7 = (f32[1,32,128]{2,1,0:T(8,128)S(1)}, f32[1,32,128]{2,1,0:T(8,128)S(1)}, u32[]{:S(2)}, u32[]{:S(2)}) collective-permute-start(f32[1,32,128]{2,1,0:T(8,128)S(1)} %get-tuple-element.376), channel_id=1, source_target_pairs={{0,1},{2,3},{4,5},{6,7},{8,9},{10,11},{12,13},{14,15},{16,17},{18,... | collective-permute-start | bytes 49160 | tf_op jit(solution)/shard_map/ppermute | solution.py:20
  314.8 7.4 %collective-permute-start.8 = (f32[34,1,128]{2,1,0:T(1,128)S(1)}, f32[34,1,128]{2,1,0:T(1,128)S(1)}, u32[]{:S(2)}, u32[]{:S(2)}) collective-permute-start(f32[34,1,128]{2,1,0:T(1,128)S(1)} %get-tuple-element.368), channel_id=1, source_target_pairs={{16,0},{32,16},{48,32},{64,48},{80,64},{96,80},{112,96},{128,112},... | collective-permute-start | bytes 52232 | tf_op jit(solution)/shard_map/ppermute | solution.py:22
  321.3 1.2 collective-permute-start.9
  325.1 3.1 collective-permute-start.10
  325.6 4.3 collective-permute-start.11
  (9 other events, 16.4 us)
Sparse Core Ops, SparseCore 0:
  290.4 158.7 all-reduce.34
where the time goes:
time: 556 us; the launch traced here: 553 us
  local copies, waits for them, and re-layouts  145 us (26%)
  waiting for transfers between devices  124 us (22%)
  blocking collectives  95.3 us (17%)
  matrix products  68.9 us (12%)
  other arithmetic  48.4 us (9%)
  starting transfers between devices  35.9 us (6%)
  between operations  29.2 us (5%)
  loops' own time  6.61 us (1%)
    psum x1, waiting for transfers between devices, body(): conv_total = lax.psum(grad_conv, ('gy', 'ga'))  113 us
    psum x1, blocking collectives, body(): lax.psum((grad_lift, grad_gain, grad_out, conv_squares), ('gx', 'gy', 'ga'))  84.4 us
    dot_general x12, matrix products, surrogate(): jnp.dot(neighbours(normed.reshape(extent_z, extent_x, extent_y, -1)), w_c...  56.3 us
    reshape x4, local copies, waits for them, and re-layouts, neighbours(): jnp.concatenate(pieces, axis=3).reshape(extent_z * extent_x * extent_y, -1)  49.7 us
    split x8, local copies, waits for them, and re-layouts, neighbours(): jnp.concatenate(pieces, axis=3).reshape(extent_z * extent_x * extent_y, -1)  28.5 us
    add_any x8, other arithmetic, neighbours(): padded[shift_z:shift_z + extent_z, shift_x:shift_x + extent_x, shift_y:sh...  17.9 us
    ppermute x6, starting transfers between devices, padded_2(): lax.ppermute(head, axis, [((i + 1) % count, i) for i in range(ends)])  16.5 us
    slice x16, local copies, waits for them, and re-layouts, neighbours(): padded[shift_z:shift_z + extent_z, shift_x:shift_x + extent_x, shift_y:sh...  16.3 us
  transfers between devices with their start and end apart: 14, of which 10 were waited for; matrix products, arithmetic and copies ran while one was open for 4% of the time, Pallas kernels for 0%

commit v1 on v0

v1 whole, which is shorter than its diff:
```python
import functools

import jax
import jax.numpy as jnp
from jax import lax
from jax.experimental import pallas as pl
from jax.experimental.pallas import tpu as pltpu
from jax.sharding import PartitionSpec as P

STEPS = 2
PVOX = 1024
CAP = 4
ROOT = 0.7978845608028654
CUBE = 0.044715
MESH = pl.DeviceIdType.MESH
f32, bf16 = jnp.float32, jnp.bfloat16


def gelu_both(v):
    v2 = v * v
    t = jnp.tanh(ROOT * (v + CUBE * (v * v2)))
    half = 0.5 * (1.0 + t)
    slope = half + 0.5 * v * (1.0 - t * t) * (ROOT * (1.0 + 3.0 * CUBE * v2))
    return v * half, slope


def z_shifted(block, z_ids):
    up = jnp.where(z_ids == 31, 0.0, pltpu.roll(block, 127, 0))
    down = jnp.where(z_ids == 0, 0.0, pltpu.roll(block, 1, 0))
    return up, down


def train_kernel(
    meta, recs, w_lift, gain, w_conv, w_out, conv_out, small_out,
    wf, wb, vp, gp, nt, nu, lifted, slope1, pre2, dh,
):
    f32, bf16 = jnp.float32, jnp.bfloat16
    vp[...] = jnp.zeros_like(vp)
    gp[...] = jnp.zeros_like(gp)
    nt[...] = jnp.zeros_like(nt)
    nu[...] = jnp.zeros_like(nu)
    conv_out[...] = jnp.zeros_like(conv_out)
    small_out[...] = jnp.zeros_like(small_out)
    for q in range(3):
        for r in range(3):
            for p in range(3):
                blk = w_conv[pl.ds(((p * 3 + q) * 3 + r) * 128, 128), :]
                wf[q * 3 + r, pl.ds(p * 128, 128), :] = blk
                wb[q * 3 + r, pl.ds(p * 128, 128), :] = blk.astype(f32).T.astype(bf16)
    z_ids = lax.broadcasted_iota(jnp.int32, (128, 128), 0) % 32
    lane = lax.broadcasted_iota(jnp.int32, (8, 128), 1)
    sub = lax.broadcasted_iota(jnp.int32, (8, 128), 0)
    gain_row = gain[...]
    wo_row = w_out[...].astype(f32)

    def patch(i, carry):
        rec = recs[i].astype(f32)
        u = rec[0:8]
        target = rec[8:16]
        for p in range(3):
            dz = p - 1
            uz = u if dz == 0 else pltpu.roll(u, (-dz) % 128, 1)
            okz = (lane % 32 + dz >= 0) & (lane % 32 + dz < 32)
            for q in range(3):
                dx = q - 1
                ux = uz if dx == 0 else pltpu.roll(uz, (-dx) % 8, 0)
                okx = (sub + dx >= 0) & (sub + dx < 8)
                for r in range(3):
                    dy = r - 1
                    uy = ux if dy == 0 else pltpu.roll(ux, (-32 * dy) % 128, 1)
                    oky = (lane // 32 + dy >= 0) & (lane // 32 + dy < 4)
                    nu[:, p * 9 + q * 3 + r, :] = jnp.where(okz & okx & oky, uy, 0.0)

        def lift(x, c):
            pre = lax.dot_general(
                nu[x].astype(bf16), w_lift[...], (((0,), (0,)), ((), ())), preferred_element_type=f32
            )
            val, slope = gelu_both(pre)
            slope1[x] = slope
            low = val.astype(bf16)
            lifted[x] = low
            wide = low.astype(f32)
            inv = lax.rsqrt(jnp.mean(wide * wide, axis=1, keepdims=True) + 1e-06)
            normed = (wide * inv * gain_row).astype(bf16).astype(f32)
            up, down = z_shifted(normed, z_ids)
            for k, v in enumerate((down, normed, up)):
                vp[x + 1, 1:5, :, k * 128 : (k + 1) * 128] = v.astype(bf16).reshape(4, 32, 128)
            nt[x + 1] = normed.T.astype(bf16)
            return c

        lax.fori_loop(0, 8, lift, 0)
        acc = None
        for q in range(3):
            for r in range(3):
                lhs = vp[q : q + 8, r : r + 4].reshape(1024, 384)
                d = jnp.dot(lhs, wf[q * 3 + r], preferred_element_type=f32)
                acc = d if acc is None else acc + d
        pre2[...] = acc

        def out_step(x, c):
            loss, dwo = c
            mixed, slope = gelu_both(pre2[pl.ds(x * 128, 128), :])
            hid = (lifted[x].astype(f32) + mixed).astype(bf16).astype(f32)
            pred = jnp.sum(hid * wo_row, axis=1, keepdims=True)
            row = jnp.sum(jnp.where(sub == x, target, 0.0), axis=0, keepdims=True)
            wanted = jnp.broadcast_to(row, (128, 128)).T
            misfit = pred - wanted
            loss = loss + jnp.sum(misfit * misfit, axis=0, keepdims=True)
            dwo = dwo + jnp.sum(hid * misfit, axis=0, keepdims=True)
            d_hid = (misfit * wo_row).astype(bf16)
            dh[x] = d_hid
            g = (d_hid.astype(f32) * slope).astype(bf16).astype(f32)
            up, down = z_shifted(g, z_ids)
            for k, v in enumerate((up, g, down)):
                gp[x + 1, 1:5, :, k * 128 : (k + 1) * 128] = v.astype(bf16).reshape(4, 32, 128)
            return loss, dwo

        zero_row = jnp.zeros((1, 128), f32)
        loss, dwo = lax.fori_loop(0, 8, out_step, (zero_row, zero_row))
        lhs = jnp.concatenate(
            [jnp.concatenate([nt[q + x] for x in range(8)], axis=1) for q in range(3)], axis=0
        )
        for r in range(3):
            rhs = gp[1:9, 2 - r : 6 - r].reshape(1024, 384)
            d = jnp.dot(lhs, rhs, preferred_element_type=f32)
            for q in range(3):
                for p in range(3):
                    rows = pl.ds(((p * 3 + q) * 3 + r) * 128, 128)
                    piece = d[q * 128 : (q + 1) * 128, p * 128 : (p + 1) * 128]
                    conv_out[rows, :] += piece.astype(bf16).astype(f32)
        acc = None
        for q in range(3):
            for r in range(3):
                lhs = gp[2 - q : 10 - q, 2 - r : 6 - r].reshape(1024, 384)
                d = jnp.dot(lhs, wb[q * 3 + r], preferred_element_type=f32)
                acc = d if acc is None else acc + d
        pre2[...] = acc

        def back(x, c):
            dgain, dwl = c
            dn = pre2[pl.ds(x * 128, 128), :].astype(bf16).astype(f32)
            wide = lifted[x].astype(f32)
            inv = lax.rsqrt(jnp.mean(wide * wide, axis=1, keepdims=True) + 1e-06)
            unit = wide * inv
            dgain = dgain + jnp.sum(dn * unit, axis=0, keepdims=True)
            dt = dn * gain_row
            mean = jnp.sum(dt * wide, axis=1, keepdims=True) * (1.0 / 128.0)
            d_low = dh[x].astype(f32) + dt * inv - (inv * inv * inv * mean) * wide
            d_pre = d_low.astype(bf16).astype(f32) * slope1[x]
            dwl = dwl + jnp.dot(nu[x].astype(bf16), d_pre.astype(bf16), preferred_element_type=f32)
            return dgain, dwl

        dgain, dwl = lax.fori_loop(0, 8, back, (zero_row, jnp.zeros((32, 128), f32)))
        small_out[0:32, :] += dwl.astype(bf16).astype(f32)
        small_out[27:28, :] += dgain
        small_out[28:29, :] += dwo.astype(bf16).astype(f32)
        small_out[32:33, :] += jnp.where(lane[0:1] == meta[1 + i, 0], 0.5 * loss, 0.0)
        return carry

    lax.fori_loop(0, meta[0, 0], patch, 0)


def lanes_of(shape):
    return lax.broadcasted_iota(jnp.int32, shape, len(shape) - 1)


def group_partners(n_gy, n_ga):
    gy, ga = lax.axis_index("gy"), lax.axis_index("ga")
    for far in range(1, n_gy * n_ga):
        there = (gy + far % n_gy) % n_gy
        across = (ga + far // n_gy) % n_ga
        yield far, {"gy": there, "ga": across}


def line_partners(n_gx):
    gx = lax.axis_index("gx")
    for far in range(1, n_gx):
        yield far, {"gx": (gx + far) % n_gx}


def meet(n_gx, n_gy, n_ga):
    barrier = pltpu.get_barrier_semaphore()
    for _, device in line_partners(n_gx):
        pl.semaphore_signal(barrier, inc=1, device_id=device, device_id_type=MESH)
    for _, device in group_partners(n_gy, n_ga):
        pl.semaphore_signal(barrier, inc=1, device_id=device, device_id_type=MESH)
    return barrier, n_gx - 1 + n_gy * n_ga - 1


def remote(src, dst, send_sem, recv_sem, device):
    return pltpu.make_async_remote_copy(
        src_ref=src, dst_ref=dst, send_sem=send_sem, recv_sem=recv_sem,
        device_id=device, device_id_type=MESH,
    )


def route_kernel(
    n_gx, n_gy, n_ga,
    count, dest, start_x, start_y, field, prev_field, diffusivity, velocity,
    new_field, batch, meta,
    state, later, prev, diff, speed, load_sem,
    mine, line, sent, group,
    z_in, x_out, x_in, y_out, y_in,
    line_send, line_recv, group_send, group_recv, halo_send, halo_recv,
):
    gx, gy, ga = lax.axis_index("gx"), lax.axis_index("gy"), lax.axis_index("ga")
    barrier, expected = meet(n_gx, n_gy, n_ga)
    size_z, size_x, size_y = prev.shape
    loads = [
        pltpu.make_async_copy(field, state.at[pl.ds(1, size_z)], load_sem.at[0]),
        pltpu.make_async_copy(prev_field, prev, load_sem.at[1]),
        pltpu.make_async_copy(diffusivity, diff, load_sem.at[2]),
        pltpu.make_async_copy(velocity, speed, load_sem.at[3]),
    ]
    for load in loads:
        load.start()
    lane8 = lanes_of((8, 128))
    xi = lax.broadcasted_iota(jnp.int32, (size_x, 128), 0)
    li = lanes_of((size_x, 128))
    row_y = lax.broadcasted_iota(jnp.int32, (128, 128), 0)
    col = lanes_of((128, 128))
    z_mask = (
        lax.broadcasted_iota(jnp.int32, (size_z, 8, 128), 0) == lanes_of((size_z, 8, 128)) % size_z
    )
    zero_tile = jnp.zeros((size_x, 128), f32)

    def pack_faces(step, cells, high, low):
        x_out[step, 0] = cells[1 : size_z + 1, 0, :]
        x_out[step, 1] = cells[1 : size_z + 1, size_x - 1, :]
        y_out[step, 0] = low
        y_out[step, 1] = high

    def halo_copies(step, cells):
        base = step * 5
        z_src = cells.at[size_z - (size_z - 1) * ga]
        there = {"ga": 1 - ga}
        z_out_copy = remote(
            z_src, z_in.at[step], halo_send.at[base], halo_recv.at[base], there
        )
        copies = [z_out_copy]
        for side in range(2):
            near = (gx + (n_gx - 1 if side == 0 else 1)) % n_gx
            copies.append(remote(
                x_out.at[step, side], x_in.at[step, 1 - side],
                halo_send.at[base + 1 + side], halo_recv.at[base + 1 + side], {"gx": near},
            ))
        for side in range(2):
            near = (gy + (n_gy - 1 if side == 0 else 1)) % n_gy
            copies.append(remote(
                y_out.at[step, side], y_in.at[step, 1 - side],
                halo_send.at[base + 3 + side], halo_recv.at[base + 3 + side], {"gy": near},
            ))
        return copies

    def place(z, cells, high, low):
        high = jnp.where(li == z, pltpu.roll(cells, z + 1, 1), high)
        low = jnp.where(li == z, pltpu.roll(cells, z, 1), low)
        return high, low

    def advance(step, cells, store, pack):
        z_face = z_in[step]
        cells[0] = jnp.where(ga == 1, z_face, 0.0)
        cells[size_z + 1] = jnp.where(ga == 0, z_face, 0.0)

        def layer(z, faces):
            centre = cells[z + 1]
            below = cells[z]
            above = cells[z + 2]
            behind = jnp.where(xi == 0, x_in[step, 0, pl.ds(z, 1), :], pltpu.roll(centre, 1, 0))
            ahead = jnp.where(
                xi == size_x - 1, x_in[step, 1, pl.ds(z, 1), :], pltpu.roll(centre, size_x - 1, 0)
            )
            left = jnp.where(
                li == 0, pltpu.roll(y_in[step, 0], 128 - z, 1), pltpu.roll(centre, 1, 1)
            )
            right = jnp.where(
                li == 127, pltpu.roll(y_in[step, 1], 127 - z, 1), pltpu.roll(centre, 127, 1)
            )
            laplace = above + below + (ahead + behind) + (right + left) - 6.0 * centre
            moved = jnp.zeros_like(centre)
            for d, (low, high) in enumerate(((below, above), (behind, ahead), (left, right))):
                v = speed[d, z]
                moved = moved + (
                    jnp.maximum(v, 0.0) * (centre - low) + jnp.minimum(v, 0.0) * (high - centre)
                )
            result = centre + diff[z] * laplace - moved
            store(z, result)
            return place(z, result, *faces) if pack else faces

        return lax.fori_loop(0, size_z, layer, (zero_tile, zero_tile))

    loads[0].wait()
    high, low = lax.fori_loop(
        0, size_z, lambda z, faces: place(z, state[z + 1], *faces), (zero_tile, zero_tile)
    )
    pack_faces(0, state, high, low)
    loads[1].wait()
    for k in range(2):
        chosen = (row_y == start_y[k] + col // size_z).astype(bf16)
        parts = []
        for source in (0, 1):
            if source == 0:
                window = prev[:, pl.ds(start_x[k], 8), :]
            else:
                window = state[1 : size_z + 1, pl.ds(start_x[k], 8), :]
            spread = jnp.dot(
                window.reshape(size_z * 8, 128).astype(bf16), chosen, preferred_element_type=f32
            ).reshape(size_z, 8, 128)
            parts.append(jnp.sum(jnp.where(z_mask, spread, 0.0), axis=0))
        mine[pl.ds(16 * k, 16), :] = jnp.concatenate(parts, axis=0).astype(bf16)
    goals = [jnp.where(k < count[0], dest[k], -1).astype(f32) for k in range(2)]
    mine[32:48, :] = jnp.concatenate(
        [jnp.full((8, 128), goals[0]), jnp.full((8, 128), goals[1])], axis=0
    ).astype(bf16)
    line[gx] = mine[...]

    pl.semaphore_wait(barrier, expected)
    first = []
    for far, device in line_partners(n_gx):
        copy = remote(mine, line.at[gx], line_send.at[far], line_recv.at[far], device)
        copy.start()
        first.append(copy)
    halos = halo_copies(0, state)
    for copy in halos:
        copy.start()

    for copy in first:
        copy.wait_recv()
    empty = jnp.zeros((16, 128), f32)
    myself = gx.astype(f32)

    def from_line(source, carry):
        rank, picked = carry
        for k in range(2):
            goal = line[source, 32:48, :].astype(f32)[8 * k : 8 * k + 8]
            record = line[source, pl.ds(16 * k, 16), :].astype(f32)
            hit = goal == myself
            picked = tuple(
                jnp.where(jnp.concatenate([hit & (rank == c)] * 2, axis=0), record, old)
                for c, old in enumerate(picked)
            )
            rank = rank + hit.astype(f32)
        return rank, picked

    rank, picked = lax.fori_loop(
        0, n_gx, from_line, (jnp.zeros((8, 128), f32), (empty,) * CAP)
    )
    for c in range(CAP):
        sent[pl.ds(16 * c, 16), :] = picked[c].astype(bf16)
    sent[16 * CAP : 16 * CAP + 16, :] = jnp.concatenate([rank, rank], axis=0).astype(bf16)
    line_id = ga * n_gy + gy
    group[line_id] = sent[...]
    second = []
    for far, device in group_partners(n_gy, n_ga):
        copy = remote(sent, group.at[line_id], group_send.at[far], group_recv.at[far], device)
        copy.start()
        second.append(copy)

    loads[2].wait()
    loads[3].wait()
    for copy in halos:
        copy.wait_recv()

    def keep(z, value):
        later[z + 1] = value

    high, low = advance(0, state, keep, True)
    pack_faces(1, later, high, low)
    more = halo_copies(1, later)
    for copy in more:
        copy.start()

    for copy in second:
        copy.wait_recv()
    share = n_gy * n_ga
    place_f = line_id.astype(f32)

    def from_group(source, carry):
        base, picked, lines = carry
        number = group[source, 16 * CAP : 16 * CAP + 16, :].astype(f32)[0:8]
        for c in range(CAP):
            record = group[source, pl.ds(16 * c, 16), :].astype(f32)
            spot = jnp.where(number > c, base + c, -1.0)
            hits = [spot == place_f + share * i for i in range(CAP)]
            picked = tuple(
                jnp.where(jnp.concatenate([hit] * 2, axis=0), record, old)
                for hit, old in zip(hits, picked)
            )
            lines = tuple(jnp.where(hit, source, old) for hit, old in zip(hits, lines))
        return base + number, picked, lines

    none = jnp.zeros((8, 128), jnp.int32)
    total, picked, lines = lax.fori_loop(
        0, share, from_group, (jnp.zeros((8, 128), f32), (empty,) * CAP, (none,) * CAP)
    )
    number = none
    for i in range(CAP):
        batch[i] = picked[i].astype(bf16)
        number = number + (place_f + share * i < total).astype(jnp.int32)
    meta[0:1, :] = number[0:1]
    for i in range(CAP):
        meta[1 + i : 2 + i, :] = lines[i][0:1]
    meta[5:8, :] = rank[0:3].astype(jnp.int32)

    for copy in more:
        copy.wait_recv()

    def emit(z, value):
        new_field[z] = value

    advance(1, later, emit, False)
    for copy in first + second + halos + more:
        copy.wait_send()


def route_call(count, dest, start_x, start_y, field, prev_field, diffusivity, velocity):
    n_gx, n_gy, n_ga = (lax.axis_size(name) for name in ("gx", "gy", "ga"))
    size_z, size_x, size_y = field.shape
    smem = pl.BlockSpec(memory_space=pltpu.SMEM)
    vmem = pl.BlockSpec(memory_space=pltpu.VMEM)
    hbm = pl.BlockSpec(memory_space=pl.ANY)
    share = n_gy * n_ga
    dma = pltpu.SemaphoreType.DMA
    return pl.pallas_call(
        functools.partial(route_kernel, n_gx, n_gy, n_ga),
        out_shape=(
            jax.ShapeDtypeStruct(field.shape, f32),
            jax.ShapeDtypeStruct((CAP, 16, 128), bf16),
            jax.ShapeDtypeStruct((8, 128), jnp.int32),
        ),
        in_specs=[smem] * 4 + [hbm] * 4,
        out_specs=(vmem,) * 3,
        scratch_shapes=[
            pltpu.VMEM((size_z + 2, size_x, size_y), f32),
            pltpu.VMEM((size_z + 2, size_x, size_y), f32),
            pltpu.VMEM((size_z, size_x, size_y), f32),
            pltpu.VMEM((size_z, size_x, size_y), f32),
            pltpu.VMEM((3, size_z, size_x, size_y), f32),
            dma((4,)),
            pltpu.VMEM((48, 128), bf16),
            pltpu.VMEM((n_gx, 48, 128), bf16),
            pltpu.VMEM((16 * CAP + 16, 128), bf16),
            pltpu.VMEM((share, 16 * CAP + 16, 128), bf16),
            pltpu.VMEM((STEPS, size_x, 128), f32),
            pltpu.VMEM((STEPS, 2, size_z, 128), f32),
            pltpu.VMEM((STEPS, 2, size_z, 128), f32),
            pltpu.VMEM((STEPS, 2, size_x, 128), f32),
            pltpu.VMEM((STEPS, 2, size_x, 128), f32),
            dma((n_gx,)),
            dma((n_gx,)),
            dma((share,)),
            dma((share,)),
            dma((STEPS * 5,)),
            dma((STEPS * 5,)),
        ],
        compiler_params=pltpu.CompilerParams(
            collective_id=0, has_side_effects=True, vmem_limit_bytes=32 * 1024 * 1024
        ),
    )(count, dest, start_x, start_y, field, prev_field, diffusivity, velocity)


def train_call(meta, recs, w_lift, gain, w_conv, w_out):
    vm = pl.BlockSpec(memory_space=pltpu.VMEM)
    return pl.pallas_call(
        train_kernel,
        out_shape=(jax.ShapeDtypeStruct((3456, 128), f32), jax.ShapeDtypeStruct((40, 128), f32)),
        in_specs=[pl.BlockSpec(memory_space=pltpu.SMEM)] + [vm] * 5,
        out_specs=(vm, vm),
        scratch_shapes=[
            pltpu.VMEM((9, 384, 128), bf16),
            pltpu.VMEM((9, 384, 128), bf16),
            pltpu.VMEM((10, 6, 32, 384), bf16),
            pltpu.VMEM((10, 6, 32, 384), bf16),
            pltpu.VMEM((10, 128, 128), bf16),
            pltpu.VMEM((8, 32, 128), f32),
            pltpu.VMEM((8, 128, 128), bf16),
            pltpu.VMEM((8, 128, 128), f32),
            pltpu.VMEM((1024, 128), f32),
            pltpu.VMEM((8, 128, 128), bf16),
        ],
        compiler_params=pltpu.CompilerParams(vmem_limit_bytes=40 * 1024 * 1024),
    )(meta, recs, w_lift, gain, w_conv, w_out)


def reduce_kernel(
    n_gx, n_gy, n_ga, rows, padded, entries,
    conv, small, meta,
    total_out, lift_out, gain_out, out_out, scale_out, loss_out,
    ring, other, gathered, pieces, from_line, tile_b, from_group, tile_c, from_all,
    ring_send, ring_recv, pair_send, pair_recv, gather_send, gather_recv,
    a_send, a_recv, b_send, b_recv, c_send, c_recv,
):
    gx, gy, ga = lax.axis_index("gx"), lax.axis_index("gy"), lax.axis_index("ga")
    line_id = ga * n_gy + gy
    barrier, expected = meet(n_gx, n_gy, n_ga)
    steps = n_gy - 1
    cut = (rows // 16) * 8
    subs = ((0, cut), (cut, rows - cut))
    cut16 = (padded // 32) * 16
    subs16 = ((0, cut16), (cut16, padded - cut16))
    signs = (1, -1)
    sub8 = lax.broadcasted_iota(jnp.int32, (8, 128), 0)
    lane8 = lanes_of((8, 128))
    share = n_gy * n_ga
    per = 32 // n_gx

    for k in range(n_gx):
        pieces[k] = jnp.concatenate(
            [small[per * k : per * k + per, :], jnp.zeros((8 - per, 128), f32)], axis=0
        )
    from_line[gx] = pieces[gx]

    def chunk_at(index, side, low, size):
        chunk = (index + 2 * n_gy) % n_gy
        start = pl.multiple_of(chunk * (2 * rows) + side * rows + low, 8)
        return pl.ds(start, size)

    def ring_copy(step, side, part):
        low, size = subs[part]
        if step == 0:
            src = conv.at[chunk_at(gy - signs[side], side, low, size)]
        else:
            src = ring.at[step - 1, side, pl.ds(low, size)]
        return remote(
            src, ring.at[step, side, pl.ds(low, size)],
            ring_send.at[step, side, part], ring_recv.at[step, side, part],
            {"gy": (gy + signs[side] + n_gy) % n_gy},
        )

    waits = []
    order = [(0, 0), (1, 0), (0, 1), (1, 1)]
    pl.semaphore_wait(barrier, expected)
    flying = {}
    for key in order:
        flying[key] = ring_copy(0, *key)
        flying[key].start()
    line_copies = []
    for far, device in line_partners(n_gx):
        copy = remote(
            pieces.at[device["gx"]], from_line.at[gx], a_send.at[far], a_recv.at[far], device
        )
        copy.start()
        line_copies.append(copy)

    for step in range(steps):
        for key in order:
            side, part = key
            low, size = subs[part]
            flying[key].wait_recv()
            waits.append(flying[key])
            mine = chunk_at(gy - signs[side] * (step + 2), side, low, size)
            ring[step, side, pl.ds(low, size), :] += conv[mine, :]
            if step + 1 < steps:
                flying[key] = ring_copy(step + 1, *key)
                flying[key].start()

    across = {"ga": 1 - ga}
    pair = remote(ring.at[steps - 1, 1 - ga], other, pair_send.at[0], pair_recv.at[0], across)
    pair.start()
    for copy in line_copies:
        copy.wait_recv()
    piece = lax.fori_loop(0, n_gx, lambda k, acc: acc + from_line[k], jnp.zeros((8, 128), f32))
    pair.wait_recv()
    total = ring[steps - 1, ga] + other[...]
    squares = jnp.sum(total * total, axis=0, keepdims=True)
    filled = [total] if padded == rows else [total, jnp.zeros((padded - rows, 128), f32)]
    gathered[gy, ga] = jnp.concatenate(filled, axis=0).astype(bf16)
    swap = remote(
        gathered.at[gy, ga], gathered.at[gy, ga], pair_send.at[1], pair_recv.at[1], across
    )
    swap.start()
    toward = 1 - 2 * ga

    def gather_copy(step, stream, part):
        low, size = subs16[part]
        sign = toward if stream == 0 else -toward
        half = ga if stream == 0 else 1 - ga
        chunk = (gy - sign * step + n_gy * 2) % n_gy
        where = gathered.at[chunk, half, pl.ds(low, size)]
        return remote(
            where, where,
            gather_send.at[step, stream, part], gather_recv.at[step, stream, part],
            {"gy": (gy + sign + n_gy) % n_gy},
        )

    for part in range(2):
        flying[0, part] = gather_copy(0, 0, part)
        flying[0, part].start()
    tile_b[...] = jnp.where(
        sub8 < per, piece, jnp.where(sub8 == per, squares, jnp.where(sub8 == per + 1, small[32:33, :], 0.0))
    )
    from_group[line_id] = tile_b[...]
    group_copies = []
    for far, device in group_partners(n_gy, n_ga):
        copy = remote(tile_b, from_group.at[line_id], b_send.at[far], b_recv.at[far], device)
        copy.start()
        group_copies.append(copy)
    swap.wait_recv()
    for part in range(2):
        flying[1, part] = gather_copy(0, 1, part)
        flying[1, part].start()

    def second_stage():
        for copy in group_copies:
            copy.wait_recv()
        summed = lax.fori_loop(
            0, share, lambda k, acc: acc + from_group[k], jnp.zeros((8, 128), f32)
        )
        tile_c[...] = summed
        from_all[gx] = summed
        copies = []
        for far, device in line_partners(n_gx):
            copy = remote(tile_c, from_all.at[gx], c_send.at[far], c_recv.at[far], device)
            copy.start()
            copies.append(copy)
        return summed, copies

    for step in range(steps):
        for stream in range(2):
            for part in range(2):
                copy = flying[stream, part]
                copy.wait_recv()
                waits.append(copy)
                if step + 1 < steps:
                    flying[stream, part] = gather_copy(step + 1, stream, part)
                    flying[stream, part].start()
        if step == min(1, steps - 1):
            summed, last_copies = second_stage()

    for copy in last_copies:
        copy.wait_recv()
    shared = jnp.concatenate([from_all[k, 0:per, :] for k in range(n_gx)], axis=0)
    conv_squares = lax.fori_loop(
        0, n_gx, lambda k, acc: acc + from_all[k], jnp.zeros((8, 128), f32)
    )[per : per + 1]
    all_squares = jnp.sum(
        conv_squares + jnp.sum(shared * shared, axis=0, keepdims=True), axis=1, keepdims=True
    )
    scale = lax.rsqrt(all_squares / entries + 1e-06)
    lift_out[...] = shared[0:27] * scale
    gain_out[...] = shared[27:28] * scale
    out_out[...] = shared[28:29] * scale
    scale_out[...] = jnp.broadcast_to(scale, (1, 128))
    number = jnp.maximum(meta[5:6, :], 1).astype(f32)
    own = jnp.sum(
        jnp.where(lane8[0:1] == line_id, summed[per + 1 : per + 2], 0.0), axis=1, keepdims=True
    )
    loss_out[...] = own / (PVOX * number)
    for chunk in range(n_gy):
        total_out[chunk] = gathered[chunk]
    for copy in waits + line_copies + group_copies + last_copies + [pair, swap]:
        copy.wait_send()


def reduce_call(conv, small, meta, entries):
    n_gx, n_gy, n_ga = (lax.axis_size(name) for name in ("gx", "gy", "ga"))
    share = n_gy * n_ga
    rows = conv.shape[0] // share
    padded = -(-rows // 16) * 16
    steps = n_gy - 1
    vmem = pl.BlockSpec(memory_space=pltpu.VMEM)
    dma = pltpu.SemaphoreType.DMA
    tile = functools.partial(jax.ShapeDtypeStruct, dtype=f32)
    return pl.pallas_call(
        functools.partial(reduce_kernel, n_gx, n_gy, n_ga, rows, padded, entries),
        out_shape=(
            jax.ShapeDtypeStruct((n_gy, n_ga, padded, 128), bf16),
            tile((27, 128)), tile((1, 128)), tile((1, 128)), tile((1, 128)), tile((1, 128)),
        ),
        in_specs=[vmem] * 3,
        out_specs=(vmem,) * 6,
        scratch_shapes=[
            pltpu.VMEM((steps, 2, rows, 128), f32),
            pltpu.VMEM((rows, 128), f32),
            pltpu.VMEM((n_gy, n_ga, padded, 128), bf16),
            pltpu.VMEM((n_gx, 8, 128), f32),
            pltpu.VMEM((n_gx, 8, 128), f32),
            pltpu.VMEM((8, 128), f32),
            pltpu.VMEM((share, 8, 128), f32),
            pltpu.VMEM((8, 128), f32),
            pltpu.VMEM((n_gx, 8, 128), f32),
            dma((steps, 2, 2)), dma((steps, 2, 2)),
            dma((2,)), dma((2,)),
            dma((steps, 2, 2)), dma((steps, 2, 2)),
            dma((n_gx,)), dma((n_gx,)),
            dma((share,)), dma((share,)),
            dma((n_gx,)), dma((n_gx,)),
        ],
        compiler_params=pltpu.CompilerParams(
            collective_id=1, has_side_effects=True, vmem_limit_bytes=32 * 1024 * 1024
        ),
    )(conv, small, meta)


def body(
    field, prev_field, diffusivity, velocity, w_lift, norm_gain, w_conv, w_out,
    tile_count, patch_dest, anchor_x, anchor_y,
):
    new_field, batch, meta = route_call(
        tile_count.reshape(1), patch_dest.reshape(2), anchor_x.reshape(2), anchor_y.reshape(2),
        field, prev_field, diffusivity, velocity,
    )
    lift_rows = jnp.pad(w_lift, ((0, 32 - w_lift.shape[0]), (0, 0)))
    conv, small = train_call(
        meta, batch, lift_rows, norm_gain[None], w_conv[0], w_out[None]
    )
    entries = w_lift.size + norm_gain.size + w_out.size + lax.axis_size("gx") * w_conv[0].size
    total, lift, gain, out, scale, loss = reduce_call(conv, small, meta, entries)
    rows = conv.shape[0] // (total.shape[0] * total.shape[1])
    dir_conv = total[:, :, :rows].astype(f32) * scale[0, 0]
    return (
        new_field, loss[:, :1].reshape(1, 1, 1), lift, gain.reshape(-1),
        dir_conv.reshape(w_conv.shape), out.reshape(-1),
    )


def solution(mesh):
    tiles = P("ga", "gx", "gy")
    slots = P("ga", "gx", "gy", None)
    in_specs = (
        tiles, tiles, tiles, P(None, "ga", "gx", "gy"), P(), P(), P("gx", None, None), P(),
        tiles, slots, slots, slots,
    )
    out_specs = (tiles, tiles, P(), P(), P("gx", None, None), P())
    return jax.shard_map(body, mesh=mesh, in_specs=in_specs, out_specs=out_specs, check_vma=False)
```

time: 556 us -> 142 us (0.26)
  the two profiles are of different devices: /device:TPU:1 before, /device:TPU:8 now
where the time goes in v1:
time: 142 us; the launch traced here: 141 us
  Pallas kernels  128 us (90%)
  local copies, waits for them, and re-layouts  9.63 us (7%)
  between operations  1.91 us (1%)
    pallas_call x1, Pallas kernels, reduce_call(): pl.pallas_call(functools.partial(reduce_kernel, n_gx, n_gy, n_ga, rows, p...  72.8 us
    pallas_call x1, Pallas kernels, route_call(): pl.pallas_call(functools.partial(route_kernel, n_gx, n_gy, n_ga), out_sha...  29.8 us
    pallas_call x1, Pallas kernels, train_call(): pl.pallas_call(train_kernel, out_shape=(jax.ShapeDtypeStruct((3456, 128),...  25.8 us
    unnamed x24, local copies, waits for them, and re-layouts  8.93 us

profile of v1, /device:TPU:8, one launch (start us, length us, event | category | flops | bytes accessed | tf_op | source)
XLA Modules:
  0.0 141.3 jit_solution(13482848537763560126)
XLA Ops:
  0.6 0.0 copy-start.6
  0.6 0.0 copy-start.5
  1.3 0.7 pad.4.w_lift
  2.0 0.0 copy-start
  2.0 1.4 copy-done
  3.4 0.0 copy-start.2
  3.4 1.0 copy-done.2
  4.5 0.0 copy-start.3
  4.5 1.0 copy-done.3
  5.5 0.0 copy-start.4
  5.5 1.0 copy-done.4
  6.6 0.0 copy-start.7
  6.6 0.7 copy-done.7
  7.2 0.0 copy-start.8
  7.2 0.7 copy-done.8
  7.9 0.0 copy-start.9
  7.9 0.7 copy-done.9
  8.5 0.0 copy-start.1
  8.5 29.8 %shard_map.163 = (f32[32,32,128]{2,1,0:T(8,128)S(1)}, bf16[4,16,128]{2,1,0:T(8,128)(2,1)S(1)}, s32[8,128]{1,0:T(8,128)S(1)}) custom-call(s32[1]{0:T(128)} %bitcast.14.count, s32[2]{0:T(128)S(1)} %bitcast.19, s32[2]{0:T(128)S(1)} %bitcast.20, s32[2]{0:T(128)S(1)} %bitcast.21, f32[32,32,128]{2,1,0:T(8,128)S(1)} %copy-done.2, f32[32,32,128]{2,1,0:T(8,128)S(1)} %copy-done.3, ...), custom_call_target="tpu_custom_call" | custom-call | tf_op jit(solution)/shard_map/pallas_call | solution.py:424
  38.4 0.0 copy-done.6
  38.4 0.0 copy-done.5
  38.4 0.0 copy-done.1
  38.4 25.8 %shard_map.164 = (f32[3456,128]{1,0:T(8,128)S(1)}, f32[40,128]{1,0:T(8,128)S(1)}) custom-call(s32[8,128]{1,0:T(8,128)S(1)} %get-tuple-element.18.meta, bf16[4,16,128]{2,1,0:T(8,128)(2,1)S(1)} %get-tuple-element.19.recs, bf16[32,128]{1,0:T(8,128)(2,1)S(1)} %pad.4.w_lift, f32[1,128]{1,0:T(1,128)S(1)} %bitcast.16, bf16[3456,128]{1,0:T(8,128)(2,1)S(1)} %bitcast.15, ...), custom_call_target="tpu_custom_call" | custom-call | tf_op jit(solution)/shard_map/pallas_call | solution.py:464
  64.2 72.8 %shard_map.165 = (bf16[8,2,224,128]{3,2,1,0:T(8,128)(2,1)S(1)}, f32[27,128]{1,0:T(8,128)S(1)}, f32[1,128]{1,0:T(1,128)S(1)}, f32[1,128]{1,0:T(1,128)S(1)}, f32[1,128]{1,0:T(1,128)S(1)}, /*index=5*/f32[1,128]{1,0:T(1,128)S(1)}) custom-call(f32[3456,128]{1,0:T(8,128)S(1)} %get-tuple-element.20.conv, f32[40,128]{1,0:T(8,128)S(1)} %get-tuple-element.21.small, ...), custom_call_target="tpu_custom_call" | custom-call | tf_op jit(solution)/shard_map/pallas_call | solution.py:664
  137.0 1.4 convert_multiply_fusion
  138.4 0.8 copy.24
  139.7 0.6 copy.26
  140.3 0.5 copy.27
  140.8 0.5 copy.28
Async XLA Ops:
  0.6 37.7 %copy-start.6 = (bf16[128]{0:T(256)(128)(2,1)S(1)}, bf16[128]{0:T(256)(128)(2,1)}, u32[]{:S(2)}) copy-start(bf16[128]{0:T(256)(128)(2,1)} %param.19) | copy-start | bytes 772
  0.6 37.7 %copy-start.5 = (f32[128]{0:T(128)S(1)}, f32[128]{0:T(128)}, u32[]{:S(2)}) copy-start(f32[128]{0:T(128)} %param.17) | copy-start | bytes 1540
  2.0 1.4 copy-start
  3.4 1.0 copy-start.2
  4.5 1.0 copy-start.3
  5.5 1.0 copy-start.4
  6.6 0.7 copy-start.7
  7.2 0.7 copy-start.8
  7.9 0.7 copy-start.9
  8.5 29.9 %copy-start.1 = (bf16[1,3456,128]{2,1,0:T(8,128)(2,1)S(1)}, bf16[1,3456,128]{2,1,0:T(8,128)(2,1)}, u32[]{:S(2)}) copy-start(bf16[1,3456,128]{2,1,0:T(8,128)(2,1)} %param.18) | copy-start | bytes 2654212

commit v2 on v1

--- a/solution.py
+++ b/solution.py
@@ -30,10 +30,18 @@
     return up, down
 
 
+def steps_of(count, step, carry):
+    for x in range(count):
+        carry = step(x, carry)
+    return carry
+
+
 def train_kernel(
-    meta, recs, w_lift, gain, w_conv, w_out, conv_out, small_out,
-    wf, wb, vp, gp, nt, nu, lifted, slope1, pre2, dh,
+    meta, recs, w_lift, gain, w_conv, w_out, cells, conv_out, small_out, cells_out,
+    wf, wb, vp, gp, nt, nu, lifted, slope1, pre2, dh, pass_sem,
 ):
+    passed = pltpu.make_async_copy(cells, cells_out, pass_sem)
+    passed.start()
     f32, bf16 = jnp.float32, jnp.bfloat16
     vp[...] = jnp.zeros_like(vp)
     gp[...] = jnp.zeros_like(gp)
@@ -88,7 +96,7 @@
             nt[x + 1] = normed.T.astype(bf16)
             return c
 
-        lax.fori_loop(0, 8, lift, 0)
+        steps_of(8, lift, 0)
         acc = None
         for q in range(3):
             for r in range(3):
@@ -116,7 +124,7 @@
             return loss, dwo
 
         zero_row = jnp.zeros((1, 128), f32)
-        loss, dwo = lax.fori_loop(0, 8, out_step, (zero_row, zero_row))
+        loss, dwo = steps_of(8, out_step, (zero_row, zero_row))
         lhs = jnp.concatenate(
             [jnp.concatenate([nt[q + x] for x in range(8)], axis=1) for q in range(3)], axis=0
         )
@@ -150,7 +158,7 @@
             dwl = dwl + jnp.dot(nu[x].astype(bf16), d_pre.astype(bf16), preferred_element_type=f32)
             return dgain, dwl
 
-        dgain, dwl = lax.fori_loop(0, 8, back, (zero_row, jnp.zeros((32, 128), f32)))
+        dgain, dwl = steps_of(8, back, (zero_row, jnp.zeros((32, 128), f32)))
         small_out[0:32, :] += dwl.astype(bf16).astype(f32)
         small_out[27:28, :] += dgain
         small_out[28:29, :] += dwo.astype(bf16).astype(f32)
@@ -158,6 +166,7 @@
         return carry
 
     lax.fori_loop(0, meta[0, 0], patch, 0)
+    passed.wait()
 
 
 def lanes_of(shape):
@@ -178,13 +187,27 @@
         yield far, {"gx": (gx + far) % n_gx}
 
 
-def meet(n_gx, n_gy, n_ga):
+def block_partners(n_ga):
+    gy, ga = lax.axis_index("gy"), lax.axis_index("ga")
+    for far in range(1, 2 * n_ga):
+        there = gy + (far % 2) * (1 - 2 * (gy % 2))
+        yield far, {"gy": there, "ga": (ga + far // 2) % n_ga}
+
+
+def meet(devices):
     barrier = pltpu.get_barrier_semaphore()
-    for _, device in line_partners(n_gx):
+    for device in devices:
         pl.semaphore_signal(barrier, inc=1, device_id=device, device_id_type=MESH)
-    for _, device in group_partners(n_gy, n_ga):
-        pl.semaphore_signal(barrier, inc=1, device_id=device, device_id_type=MESH)
-    return barrier, n_gx - 1 + n_gy * n_ga - 1
+    return barrier, len(devices)
+
+
+def several(count, step, carry, at_once=4):
+    def run(block, carry):
+        for i in range(at_once):
+            carry = step(block * at_once + i, carry)
+        return carry
+
+    return lax.fori_loop(0, count // at_once, run, carry)
 
 
 def remote(src, dst, send_sem, recv_sem, device):
@@ -204,7 +227,11 @@
     line_send, line_recv, group_send, group_recv, halo_send, halo_recv,
 ):
     gx, gy, ga = lax.axis_index("gx"), lax.axis_index("gy"), lax.axis_index("ga")
-    barrier, expected = meet(n_gx, n_gy, n_ga)
+    barrier, expected = meet(
+        [device for _, device in line_partners(n_gx)]
+        + [device for _, device in block_partners(n_ga)]
+        + [{"gy": (gy + 1) % n_gy}, {"gy": (gy + n_gy - 1) % n_gy}]
+    )
     size_z, size_x, size_y = prev.shape
     loads = [
         pltpu.make_async_copy(field, state.at[pl.ds(1, size_z)], load_sem.at[0]),
@@ -287,11 +314,11 @@
             store(z, result)
             return place(z, result, *faces) if pack else faces
 
-        return lax.fori_loop(0, size_z, layer, (zero_tile, zero_tile))
+        return several(size_z, layer, (zero_tile, zero_tile))
 
     loads[0].wait()
-    high, low = lax.fori_loop(
-        0, size_z, lambda z, faces: place(z, state[z + 1], *faces), (zero_tile, zero_tile)
+    high, low = several(
+        size_z, lambda z, faces: place(z, state[z + 1], *faces), (zero_tile, zero_tile)
     )
     pack_faces(0, state, high, low)
     loads[1].wait()
@@ -324,6 +351,20 @@
     for copy in halos:
         copy.start()
 
+    loads[2].wait()
+    loads[3].wait()
+    for copy in halos:
+        copy.wait_recv()
+
+    def keep(z, value):
+        later[z + 1] = value
+
+    high, low = advance(0, state, keep, True)
+    pack_faces(1, later, high, low)
+    more = halo_copies(1, later)
+    for copy in more:
+        copy.start()
+
     for copy in first:
         copy.wait_recv()
     empty = jnp.zeros((16, 128), f32)
@@ -348,32 +389,26 @@
     for c in range(CAP):
         sent[pl.ds(16 * c, 16), :] = picked[c].astype(bf16)
     sent[16 * CAP : 16 * CAP + 16, :] = jnp.concatenate([rank, rank], axis=0).astype(bf16)
-    line_id = ga * n_gy + gy
-    group[line_id] = sent[...]
+    place_id = ga * 2 + gy % 2
+    group[place_id] = sent[...]
     second = []
-    for far, device in group_partners(n_gy, n_ga):
-        copy = remote(sent, group.at[line_id], group_send.at[far], group_recv.at[far], device)
+    for far, device in block_partners(n_ga):
+        copy = remote(sent, group.at[place_id], group_send.at[far], group_recv.at[far], device)
         copy.start()
         second.append(copy)
 
-    loads[2].wait()
-    loads[3].wait()
-    for copy in halos:
+    for copy in more:
         copy.wait_recv()
 
-    def keep(z, value):
-        later[z + 1] = value
-
-    high, low = advance(0, state, keep, True)
-    pack_faces(1, later, high, low)
-    more = halo_copies(1, later)
-    for copy in more:
-        copy.start()
-
+    def emit(z, value):
+        new_field[z] = value
+
+    advance(1, later, emit, False)
     for copy in second:
         copy.wait_recv()
-    share = n_gy * n_ga
-    place_f = line_id.astype(f32)
+    share = 2 * n_ga
+    place_f = place_id.astype(f32)
+    first_line = gy - gy % 2
 
     def from_group(source, carry):
         base, picked, lines = carry
@@ -386,7 +421,8 @@
                 jnp.where(jnp.concatenate([hit] * 2, axis=0), record, old)
                 for hit, old in zip(hits, picked)
             )
-            lines = tuple(jnp.where(hit, source, old) for hit, old in zip(hits, lines))
+            origin = (source // 2) * n_gy + first_line + source % 2
+            lines = tuple(jnp.where(hit, origin, old) for hit, old in zip(hits, lines))
         return base + number, picked, lines
 
     none = jnp.zeros((8, 128), jnp.int32)
@@ -402,13 +438,6 @@
         meta[1 + i : 2 + i, :] = lines[i][0:1]
     meta[5:8, :] = rank[0:3].astype(jnp.int32)
 
-    for copy in more:
-        copy.wait_recv()
-
-    def emit(z, value):
-        new_field[z] = value
-
-    advance(1, later, emit, False)
     for copy in first + second + halos + more:
         copy.wait_send()
 
@@ -418,8 +447,8 @@
     size_z, size_x, size_y = field.shape
     smem = pl.BlockSpec(memory_space=pltpu.SMEM)
     vmem = pl.BlockSpec(memory_space=pltpu.VMEM)
-    hbm = pl.BlockSpec(memory_space=pl.ANY)
-    share = n_gy * n_ga
+    hbm = pl.BlockSpec(memory_space=pltpu.HBM)
+    share = 2 * n_ga
     dma = pltpu.SemaphoreType.DMA
     return pl.pallas_call(
         functools.partial(route_kernel, n_gx, n_gy, n_ga),
@@ -454,18 +483,23 @@
             dma((STEPS * 5,)),
         ],
         compiler_params=pltpu.CompilerParams(
-            collective_id=0, has_side_effects=True, vmem_limit_bytes=32 * 1024 * 1024
+            collective_id=0, has_side_effects=True, vmem_limit_bytes=56 * 1024 * 1024
         ),
     )(count, dest, start_x, start_y, field, prev_field, diffusivity, velocity)
 
 
-def train_call(meta, recs, w_lift, gain, w_conv, w_out):
+def train_call(meta, recs, w_lift, gain, w_conv, w_out, cells):
     vm = pl.BlockSpec(memory_space=pltpu.VMEM)
+    hbm = pl.BlockSpec(memory_space=pltpu.HBM)
     return pl.pallas_call(
         train_kernel,
-        out_shape=(jax.ShapeDtypeStruct((3456, 128), f32), jax.ShapeDtypeStruct((40, 128), f32)),
-        in_specs=[pl.BlockSpec(memory_space=pltpu.SMEM)] + [vm] * 5,
-        out_specs=(vm, vm),
+        out_shape=(
+            jax.ShapeDtypeStruct((3456, 128), f32),
+            jax.ShapeDtypeStruct((40, 128), f32),
+            jax.ShapeDtypeStruct(cells.shape, f32),
+        ),
+        in_specs=[pl.BlockSpec(memory_space=pltpu.SMEM)] + [vm] * 6,
+        out_specs=(vm, vm, hbm),
         scratch_shapes=[
             pltpu.VMEM((9, 384, 128), bf16),
             pltpu.VMEM((9, 384, 128), bf16),
@@ -477,28 +511,37 @@
             pltpu.VMEM((8, 128, 128), f32),
             pltpu.VMEM((1024, 128), f32),
             pltpu.VMEM((8, 128, 128), bf16),
+            pltpu.SemaphoreType.DMA,
         ],
-        compiler_params=pltpu.CompilerParams(vmem_limit_bytes=40 * 1024 * 1024),
-    )(meta, recs, w_lift, gain, w_conv, w_out)
+        compiler_params=pltpu.CompilerParams(vmem_limit_bytes=32 * 1024 * 1024),
+    )(meta, recs, w_lift, gain, w_conv, w_out, cells)
+
+
+def row_cuts(rows):
+    tiles = rows // 16
+    ends = [16 * (tiles * i // 4 + (1 if 0 < i < 4 and tiles * i % 4 else 0)) for i in range(5)]
+    return [(low, high - low) for low, high in zip(ends, ends[1:])]
 
 
 def reduce_kernel(
-    n_gx, n_gy, n_ga, rows, padded, entries,
+    n_gx, n_gy, n_ga, rows, entries,
     conv, small, meta,
-    total_out, lift_out, gain_out, out_out, scale_out, loss_out,
-    ring, other, gathered, pieces, from_line, tile_b, from_group, tile_c, from_all,
+    total_out, tail_out,
+    ring, own, other, gathered, pieces, from_line, tile_b, from_group, tile_c, from_all,
     ring_send, ring_recv, pair_send, pair_recv, gather_send, gather_recv,
     a_send, a_recv, b_send, b_recv, c_send, c_recv,
 ):
     gx, gy, ga = lax.axis_index("gx"), lax.axis_index("gy"), lax.axis_index("ga")
     line_id = ga * n_gy + gy
-    barrier, expected = meet(n_gx, n_gy, n_ga)
-    steps = n_gy - 1
-    cut = (rows // 16) * 8
-    subs = ((0, cut), (cut, rows - cut))
-    cut16 = (padded // 32) * 16
-    subs16 = ((0, cut16), (cut16, padded - cut16))
+    barrier, expected = meet(
+        [device for _, device in line_partners(n_gx)]
+        + [device for _, device in group_partners(n_gy, n_ga)]
+    )
+    subs = row_cuts(rows)
+    far_side = n_gy // 2
     signs = (1, -1)
+    keys = [(0, 0), (1, 2), (0, 1), (1, 3), (0, 2), (1, 0), (0, 3), (1, 1)]
+    depth = {(side, part): far_side if part // 2 == side else n_gy - 1 - far_side for side, part in keys}
     sub8 = lax.broadcasted_iota(jnp.int32, (8, 128), 0)
     lane8 = lanes_of((8, 128))
     share = n_gy * n_ga
@@ -510,123 +553,121 @@
         )
     from_line[gx] = pieces[gx]
 
-    def chunk_at(index, side, low, size):
-        chunk = (index + 2 * n_gy) % n_gy
-        start = pl.multiple_of(chunk * (2 * rows) + side * rows + low, 8)
-        return pl.ds(start, size)
+    def wrap(index):
+        return (index + 2 * n_gy) % n_gy
+
+    def rows_of(index, part):
+        low, size = subs[part]
+        return pl.ds(pl.multiple_of(wrap(index) * rows + low, 8), size)
+
+    def next_to(side):
+        return {"gy": wrap(gy + signs[side])}
 
     def ring_copy(step, side, part):
         low, size = subs[part]
         if step == 0:
-            src = conv.at[chunk_at(gy - signs[side], side, low, size)]
+            src = conv.at[rows_of(gy + signs[side] * depth[side, part], part)]
         else:
             src = ring.at[step - 1, side, pl.ds(low, size)]
         return remote(
             src, ring.at[step, side, pl.ds(low, size)],
-            ring_send.at[step, side, part], ring_recv.at[step, side, part],
-            {"gy": (gy + signs[side] + n_gy) % n_gy},
+            ring_send.at[step, side, part], ring_recv.at[step, side, part], next_to(side),
         )
 
-    waits = []
-    order = [(0, 0), (1, 0), (0, 1), (1, 1)]
+    started = []
+
+    def begin(copy):
+        copy.start()
+        started.append(copy)
+        return copy
+
     pl.semaphore_wait(barrier, expected)
-    flying = {}
-    for key in order:
-        flying[key] = ring_copy(0, *key)
-        flying[key].start()
-    line_copies = []
-    for far, device in line_partners(n_gx):
-        copy = remote(
+    flying = {key: begin(ring_copy(0, *key)) for key in keys}
+    line_copies = [
+        begin(remote(
             pieces.at[device["gx"]], from_line.at[gx], a_send.at[far], a_recv.at[far], device
-        )
-        copy.start()
-        line_copies.append(copy)
-
-    for step in range(steps):
-        for key in order:
+        ))
+        for far, device in line_partners(n_gx)
+    ]
+
+    pairs = {}
+    for step in range(far_side):
+        for key in keys:
             side, part = key
             low, size = subs[part]
+            if step >= depth[key]:
+                continue
             flying[key].wait_recv()
-            waits.append(flying[key])
-            mine = chunk_at(gy - signs[side] * (step + 2), side, low, size)
-            ring[step, side, pl.ds(low, size), :] += conv[mine, :]
-            if step + 1 < steps:
-                flying[key] = ring_copy(step + 1, *key)
-                flying[key].start()
-
-    across = {"ga": 1 - ga}
-    pair = remote(ring.at[steps - 1, 1 - ga], other, pair_send.at[0], pair_recv.at[0], across)
-    pair.start()
+            if step + 1 < depth[key]:
+                there = rows_of(gy + signs[side] * (depth[key] - 1 - step), part)
+                ring[step, side, pl.ds(low, size), :] += conv[there, :]
+                flying[key] = begin(ring_copy(step + 1, *key))
+            elif step == far_side - 1:
+                here = pl.ds(low, size)
+                near = depth[1 - side, part] - 1
+                own[here, :] = (
+                    ring[step, side, here, :] + ring[near, 1 - side, here, :]
+                ) + conv[rows_of(gy, part), :]
+                pairs[part] = begin(remote(
+                    own.at[here], other.at[here], pair_send.at[part], pair_recv.at[part],
+                    {"ga": 1 - ga},
+                ))
+
     for copy in line_copies:
         copy.wait_recv()
     piece = lax.fori_loop(0, n_gx, lambda k, acc: acc + from_line[k], jnp.zeros((8, 128), f32))
-    pair.wait_recv()
-    total = ring[steps - 1, ga] + other[...]
-    squares = jnp.sum(total * total, axis=0, keepdims=True)
-    filled = [total] if padded == rows else [total, jnp.zeros((padded - rows, 128), f32)]
-    gathered[gy, ga] = jnp.concatenate(filled, axis=0).astype(bf16)
-    swap = remote(
-        gathered.at[gy, ga], gathered.at[gy, ga], pair_send.at[1], pair_recv.at[1], across
-    )
-    swap.start()
-    toward = 1 - 2 * ga
-
-    def gather_copy(step, stream, part):
-        low, size = subs16[part]
-        sign = toward if stream == 0 else -toward
-        half = ga if stream == 0 else 1 - ga
-        chunk = (gy - sign * step + n_gy * 2) % n_gy
-        where = gathered.at[chunk, half, pl.ds(low, size)]
+
+    def gather_copy(step, side, part):
+        low, size = subs[part]
+        where = gathered.at[wrap(gy - signs[side] * step), pl.ds(low, size)]
         return remote(
             where, where,
-            gather_send.at[step, stream, part], gather_recv.at[step, stream, part],
-            {"gy": (gy + sign + n_gy) % n_gy},
+            gather_send.at[step, side, part], gather_recv.at[step, side, part], next_to(side),
         )
 
-    for part in range(2):
-        flying[0, part] = gather_copy(0, 0, part)
-        flying[0, part].start()
+    squares = jnp.zeros((1, 128), f32)
+    for part in (0, 2, 1, 3):
+        low, size = subs[part]
+        here = pl.ds(low, size)
+        pairs[part].wait_recv()
+        total = own[here, :] + other[here, :]
+        gathered[gy, here, :] = total.astype(bf16)
+        for side in (part // 2, 1 - part // 2):
+            flying[side, part] = begin(gather_copy(0, side, part))
+        squares = squares + jnp.sum(total * total, axis=0, keepdims=True)
+    squares = jnp.where(ga == 0, squares, 0.0)
     tile_b[...] = jnp.where(
-        sub8 < per, piece, jnp.where(sub8 == per, squares, jnp.where(sub8 == per + 1, small[32:33, :], 0.0))
+        sub8 < per,
+        piece,
+        jnp.where(sub8 == per, squares, jnp.where(sub8 == per + 1, small[32:33, :], 0.0)),
     )
     from_group[line_id] = tile_b[...]
-    group_copies = []
-    for far, device in group_partners(n_gy, n_ga):
-        copy = remote(tile_b, from_group.at[line_id], b_send.at[far], b_recv.at[far], device)
-        copy.start()
-        group_copies.append(copy)
-    swap.wait_recv()
-    for part in range(2):
-        flying[1, part] = gather_copy(0, 1, part)
-        flying[1, part].start()
-
-    def second_stage():
-        for copy in group_copies:
-            copy.wait_recv()
-        summed = lax.fori_loop(
-            0, share, lambda k, acc: acc + from_group[k], jnp.zeros((8, 128), f32)
-        )
-        tile_c[...] = summed
-        from_all[gx] = summed
-        copies = []
-        for far, device in line_partners(n_gx):
-            copy = remote(tile_c, from_all.at[gx], c_send.at[far], c_recv.at[far], device)
-            copy.start()
-            copies.append(copy)
-        return summed, copies
-
-    for step in range(steps):
-        for stream in range(2):
-            for part in range(2):
-                copy = flying[stream, part]
+    group_copies = [
+        begin(remote(tile_b, from_group.at[line_id], b_send.at[far], b_recv.at[far], device))
+        for far, device in group_partners(n_gy, n_ga)
+    ]
+
+    for step in range(far_side):
+        for key in keys:
+            if step >= depth[key]:
+                continue
+            flying[key].wait_recv()
+            if step + 1 < depth[key]:
+                flying[key] = begin(gather_copy(step + 1, *key))
+        if step == 1:
+            for copy in group_copies:
                 copy.wait_recv()
-                waits.append(copy)
-                if step + 1 < steps:
-                    flying[stream, part] = gather_copy(step + 1, stream, part)
-                    flying[stream, part].start()
-        if step == min(1, steps - 1):
-            summed, last_copies = second_stage()
-
+            summed = lax.fori_loop(
+                0, share, lambda k, acc: acc + from_group[k], jnp.zeros((8, 128), f32)
+            )
+            tile_c[...] = summed
+            from_all[gx] = summed
+            last_copies = [
+                begin(remote(tile_c, from_all.at[gx], c_send.at[far], c_recv.at[far], device))
+                for far, device in line_partners(n_gx)
+            ]
+
+    total_out[...] = gathered[...]
     for copy in last_copies:
         copy.wait_recv()
     shared = jnp.concatenate([from_all[k, 0:per, :] for k in range(n_gx)], axis=0)
@@ -637,51 +678,45 @@
         conv_squares + jnp.sum(shared * shared, axis=0, keepdims=True), axis=1, keepdims=True
     )
     scale = lax.rsqrt(all_squares / entries + 1e-06)
-    lift_out[...] = shared[0:27] * scale
-    gain_out[...] = shared[27:28] * scale
-    out_out[...] = shared[28:29] * scale
-    scale_out[...] = jnp.broadcast_to(scale, (1, 128))
+    tail_out[0:32, :] = shared * scale
     number = jnp.maximum(meta[5:6, :], 1).astype(f32)
-    own = jnp.sum(
+    own_loss = jnp.sum(
         jnp.where(lane8[0:1] == line_id, summed[per + 1 : per + 2], 0.0), axis=1, keepdims=True
     )
-    loss_out[...] = own / (PVOX * number)
-    for chunk in range(n_gy):
-        total_out[chunk] = gathered[chunk]
-    for copy in waits + line_copies + group_copies + last_copies + [pair, swap]:
+    loss = own_loss / (PVOX * number)
+    tail_out[32:40, :] = jnp.where(sub8 == 0, jnp.broadcast_to(scale, (8, 128)), loss)
+    for copy in started:
         copy.wait_send()
 
 
 def reduce_call(conv, small, meta, entries):
     n_gx, n_gy, n_ga = (lax.axis_size(name) for name in ("gx", "gy", "ga"))
     share = n_gy * n_ga
-    rows = conv.shape[0] // share
-    padded = -(-rows // 16) * 16
-    steps = n_gy - 1
+    rows = conv.shape[0] // n_gy
+    far_side = n_gy // 2
     vmem = pl.BlockSpec(memory_space=pltpu.VMEM)
     dma = pltpu.SemaphoreType.DMA
-    tile = functools.partial(jax.ShapeDtypeStruct, dtype=f32)
     return pl.pallas_call(
-        functools.partial(reduce_kernel, n_gx, n_gy, n_ga, rows, padded, entries),
+        functools.partial(reduce_kernel, n_gx, n_gy, n_ga, rows, entries),
         out_shape=(
-            jax.ShapeDtypeStruct((n_gy, n_ga, padded, 128), bf16),
-            tile((27, 128)), tile((1, 128)), tile((1, 128)), tile((1, 128)), tile((1, 128)),
+            jax.ShapeDtypeStruct((n_gy, rows, 128), bf16), jax.ShapeDtypeStruct((40, 128), f32)
         ),
         in_specs=[vmem] * 3,
-        out_specs=(vmem,) * 6,
+        out_specs=(vmem,) * 2,
         scratch_shapes=[
-            pltpu.VMEM((steps, 2, rows, 128), f32),
+            pltpu.VMEM((far_side, 2, rows, 128), f32),
             pltpu.VMEM((rows, 128), f32),
-            pltpu.VMEM((n_gy, n_ga, padded, 128), bf16),
+            pltpu.VMEM((rows, 128), f32),
+            pltpu.VMEM((n_gy, rows, 128), bf16),
             pltpu.VMEM((n_gx, 8, 128), f32),
             pltpu.VMEM((n_gx, 8, 128), f32),
             pltpu.VMEM((8, 128), f32),
             pltpu.VMEM((share, 8, 128), f32),
             pltpu.VMEM((8, 128), f32),
             pltpu.VMEM((n_gx, 8, 128), f32),
-            dma((steps, 2, 2)), dma((steps, 2, 2)),
-            dma((2,)), dma((2,)),
-            dma((steps, 2, 2)), dma((steps, 2, 2)),
+            dma((far_side, 2, 4)), dma((far_side, 2, 4)),
+            dma((4,)), dma((4,)),
+            dma((far_side, 2, 4)), dma((far_side, 2, 4)),
             dma((n_gx,)), dma((n_gx,)),
             dma((share,)), dma((share,)),
             dma((n_gx,)), dma((n_gx,)),
@@ -692,22 +727,47 @@
     )(conv, small, meta)
 
 
+def finish_kernel(total, tail, conv_out, lift_out, gain_out, out_out, loss_out):
+    scale = tail[32:33, :]
+    for chunk in range(total.shape[0]):
+        size = total.shape[1]
+        conv_out[pl.ds(chunk * size, size), :] = total[chunk].astype(f32) * scale
+    lift_out[...] = tail[0:27, :]
+    gain_out[...] = tail[27:28, :]
+    out_out[...] = tail[28:29, :]
+    loss_out[...] = tail[33:34, :]
+
+
+def finish_call(total, tail):
+    vmem = pl.BlockSpec(memory_space=pltpu.VMEM)
+    tile = functools.partial(jax.ShapeDtypeStruct, dtype=f32)
+    return pl.pallas_call(
+        finish_kernel,
+        out_shape=(
+            tile((total.shape[0] * total.shape[1], 128)),
+            tile((27, 128)), tile((1, 128)), tile((1, 128)), tile((1, 128)),
+        ),
+        in_specs=[vmem] * 2,
+        out_specs=(vmem,) * 5,
+        compiler_params=pltpu.CompilerParams(vmem_limit_bytes=16 * 1024 * 1024),
+    )(total, tail)
+
+
 def body(
     field, prev_field, diffusivity, velocity, w_lift, norm_gain, w_conv, w_out,
     tile_count, patch_dest, anchor_x, anchor_y,
 ):
-    new_field, batch, meta = route_call(
+    stepped, batch, meta = route_call(
         tile_count.reshape(1), patch_dest.reshape(2), anchor_x.reshape(2), anchor_y.reshape(2),
         field, prev_field, diffusivity, velocity,
     )
     lift_rows = jnp.pad(w_lift, ((0, 32 - w_lift.shape[0]), (0, 0)))
-    conv, small = train_call(
-        meta, batch, lift_rows, norm_gain[None], w_conv[0], w_out[None]
+    conv, small, new_field = train_call(
+        meta, batch, lift_rows, norm_gain[None], w_conv[0], w_out[None], stepped
     )
     entries = w_lift.size + norm_gain.size + w_out.size + lax.axis_size("gx") * w_conv[0].size
-    total, lift, gain, out, scale, loss = reduce_call(conv, small, meta, entries)
-    rows = conv.shape[0] // (total.shape[0] * total.shape[1])
-    dir_conv = total[:, :, :rows].astype(f32) * scale[0, 0]
+    total, tail = reduce_call(conv, small, meta, entries)
+    dir_conv, lift, gain, out, loss = finish_call(total, tail)
     return (
         new_field, loss[:, :1].reshape(1, 1, 1), lift, gain.reshape(-1),
         dir_conv.reshape(w_conv.shape), out.reshape(-1),

time: 142 us -> 92.8 us (0.65)
  the two profiles are of different devices: /device:TPU:8 before, /device:TPU:1 now
where the time goes in v2:
time: 92.8 us; the launch traced here: 92.5 us
  Pallas kernels  87.9 us (95%)
  local copies, waits for them, and re-layouts  3.15 us (3%)
  between operations  1.44 us (2%)
    pallas_call x1, Pallas kernels, reduce_call(): pl.pallas_call(functools.partial(reduce_kernel, n_gx, n_gy, n_ga, rows, e...  49.1 us
    pallas_call x1, Pallas kernels, route_call(): pl.pallas_call(functools.partial(route_kernel, n_gx, n_gy, n_ga), out_sha...  22.8 us
    pallas_call x1, Pallas kernels, train_call(): pl.pallas_call(train_kernel, out_shape=(jax.ShapeDtypeStruct((3456, 128),...  14.7 us
    unnamed x12, local copies, waits for them, and re-layouts  2.45 us

profile of v2, /device:TPU:1, one launch (start us, length us, event | category | flops | bytes accessed | tf_op | source)
XLA Modules:
  0.0 92.5 jit_solution(11879950841376513977)
XLA Ops:
  0.6 0.0 copy-start.5
  0.6 0.0 copy-start
  0.7 0.0 copy-start.4
  1.4 0.7 pad.4.w_lift
  2.1 22.8 %shard_map.163 = (f32[32,32,128]{2,1,0:T(8,128)}, bf16[4,16,128]{2,1,0:T(8,128)(2,1)}, s32[8,128]{1,0:T(8,128)}) custom-call(s32[1]{0:T(128)} %bitcast.12.count, s32[2]{0:T(128)} %bitcast.16, s32[2]{0:T(128)} %bitcast.17, s32[2]{0:T(128)} %bitcast.18, f32[32,32,128]{2,1,0:T(8,128)} %field.1, f32[32,32,128]{2,1,0:T(8,128)} %prev_field.1, ...), custom_call_target="tpu_custom_call" | custom-call | tf_op jit(solution)/shard_map/pallas_call | solution.py:453
  24.9 0.0 copy-done.5
  24.9 0.0 copy-done
  24.9 0.0 copy-done.4
  24.9 0.0 copy-start.1
  24.9 1.0 %copy-done.1 = f32[32,32,128]{2,1,0:T(8,128)S(1)} copy-done((f32[32,32,128]{2,1,0:T(8,128)S(1)}, f32[32,32,128]{2,1,0:T(8,128)}, u32[]{:S(2)}) %copy-start.1) | copy-done | bytes 524312
  25.9 0.0 copy-start.2
  25.9 0.7 copy-done.2
  26.7 0.0 copy-start.3
  26.7 0.7 copy-done.3
  27.3 14.7 %shard_map.164 = (f32[3456,128]{1,0:T(8,128)S(1)}, f32[40,128]{1,0:T(8,128)S(1)}, f32[32,32,128]{2,1,0:T(8,128)}) custom-call(s32[8,128]{1,0:T(8,128)S(1)} %copy-done.3, bf16[4,16,128]{2,1,0:T(8,128)(2,1)S(1)} %copy-done.2, bf16[32,128]{1,0:T(8,128)(2,1)S(1)} %pad.4.w_lift, f32[1,128]{1,0:T(1,128)S(1)} %bitcast.14, bf16[3456,128]{1,0:T(8,128)(2,1)S(1)} %bitcast.13, ...), custom_call_target="tpu_custom_call" | custom-call | tf_op jit(solution)/shard_map/pallas_call | solution.py:494
  42.0 49.1 %shard_map.165 = (bf16[8,432,128]{2,1,0:T(8,128)(2,1)S(1)}, f32[40,128]{1,0:T(8,128)S(1)}) custom-call(f32[3456,128]{1,0:T(8,128)S(1)} %get-tuple-element.23.conv, f32[40,128]{1,0:T(8,128)S(1)} %get-tuple-element.24.small, s32[8,128]{1,0:T(8,128)S(1)} %copy-done.3), custom_call_target="tpu_custom_call" | custom-call | tf_op jit(solution)/shard_map/pallas_call | solution.py:699
  91.2 1.3 %shard_map.166 = (f32[3456,128]{1,0:T(8,128)}, f32[27,128]{1,0:T(8,128)}, f32[1,128]{1,0:T(1,128)}, f32[1,128]{1,0:T(1,128)}, f32[1,128]{1,0:T(1,128)}) custom-call(bf16[8,432,128]{2,1,0:T(8,128)(2,1)S(1)} %get-tuple-element.25.total, f32[40,128]{1,0:T(8,128)S(1)} %get-tuple-element.26.tail), custom_call_target="tpu_custom_call" | custom-call | tf_op jit(solution)/shard_map/pallas_call | solution.py:744
Async XLA Ops:
  0.6 24.2 %copy-start.5 = (bf16[128]{0:T(256)(128)(2,1)S(1)}, bf16[128]{0:T(256)(128)(2,1)}, u32[]{:S(2)}) copy-start(bf16[128]{0:T(256)(128)(2,1)} %param.19) | copy-start | bytes 772
  0.6 24.2 %copy-start = (bf16[1,3456,128]{2,1,0:T(8,128)(2,1)S(1)}, bf16[1,3456,128]{2,1,0:T(8,128)(2,1)}, u32[]{:S(2)}) copy-start(bf16[1,3456,128]{2,1,0:T(8,128)(2,1)} %param.18) | copy-start | bytes 2654212
  0.7 24.2 %copy-start.4 = (f32[128]{0:T(128)S(1)}, f32[128]{0:T(128)}, u32[]{:S(2)}) copy-start(f32[128]{0:T(128)} %param.17) | copy-start | bytes 1540
  24.9 1.0 %copy-start.1 = (f32[32,32,128]{2,1,0:T(8,128)S(1)}, f32[32,32,128]{2,1,0:T(8,128)}, u32[]{:S(2)}) copy-start(f32[32,32,128]{2,1,0:T(8,128)} %get-tuple-element.21.cells) | copy-start | bytes 1572868
  25.9 0.7 copy-start.2
  26.7 0.7 copy-start.3

commit v3 on v2

--- a/solution.py
+++ b/solution.py
@@ -10,6 +10,7 @@
 STEPS = 2
 PVOX = 1024
 CAP = 4
+META = 16 * CAP
 ROOT = 0.7978845608028654
 CUBE = 0.044715
 MESH = pl.DeviceIdType.MESH
@@ -36,12 +37,32 @@
     return carry
 
 
+def move_y(block, by):
+    if by == 0:
+        return block
+    gap = jnp.zeros((1,) + block.shape[1:], block.dtype)
+    parts = [block[1:], gap] if by > 0 else [gap, block[:-1]]
+    return jnp.concatenate(parts, axis=0)
+
+
+def conv_rows(source, weights, x, sign):
+    acc = None
+    for q in range(3):
+        x_in = x + sign * (q - 1)
+        if x_in < 0 or x_in > 7:
+            continue
+        lhs = source[x_in + 1, 1:5].reshape(128, 384)
+        d = jnp.dot(lhs, weights[q], preferred_element_type=f32).reshape(4, 32, 384)
+        for r in range(3):
+            piece = move_y(d[:, :, r * 128 : (r + 1) * 128], sign * (r - 1))
+            acc = piece if acc is None else acc + piece
+    return acc.reshape(128, 128)
+
+
 def train_kernel(
-    meta, recs, w_lift, gain, w_conv, w_out, cells, conv_out, small_out, cells_out,
-    wf, wb, vp, gp, nt, nu, lifted, slope1, pre2, dh, pass_sem,
+    routed, w_lift, gain, w_conv, w_out, conv_out, small_out,
+    wf, wb, vp, gp, nt, nu, lifted, slope1, pre2, dh, lift_rows,
 ):
-    passed = pltpu.make_async_copy(cells, cells_out, pass_sem)
-    passed.start()
     f32, bf16 = jnp.float32, jnp.bfloat16
     vp[...] = jnp.zeros_like(vp)
     gp[...] = jnp.zeros_like(gp)
@@ -53,18 +74,20 @@
         for r in range(3):
             for p in range(3):
                 blk = w_conv[pl.ds(((p * 3 + q) * 3 + r) * 128, 128), :]
-                wf[q * 3 + r, pl.ds(p * 128, 128), :] = blk
-                wb[q * 3 + r, pl.ds(p * 128, 128), :] = blk.astype(f32).T.astype(bf16)
+                wf[q, pl.ds(p * 128, 128), pl.ds(r * 128, 128)] = blk
+                wb[q, pl.ds(p * 128, 128), pl.ds(r * 128, 128)] = blk.astype(f32).T.astype(bf16)
     z_ids = lax.broadcasted_iota(jnp.int32, (128, 128), 0) % 32
     lane = lax.broadcasted_iota(jnp.int32, (8, 128), 1)
     sub = lax.broadcasted_iota(jnp.int32, (8, 128), 0)
     gain_row = gain[...]
+    lift_rows[...] = jnp.zeros_like(lift_rows)
+    lift_rows[0:27, :] = w_lift[...].astype(f32)
+    lift_weights = lift_rows[...].astype(bf16)
     wo_row = w_out[...].astype(f32)
 
     def patch(i, carry):
-        rec = recs[i].astype(f32)
-        u = rec[0:8]
-        target = rec[8:16]
+        u = routed[pl.ds(16 * i, 8), :]
+        target = routed[pl.ds(16 * i + 8, 8), :]
         for p in range(3):
             dz = p - 1
             uz = u if dz == 0 else pltpu.roll(u, (-dz) % 128, 1)
@@ -81,7 +104,7 @@
 
         def lift(x, c):
             pre = lax.dot_general(
-                nu[x].astype(bf16), w_lift[...], (((0,), (0,)), ((), ())), preferred_element_type=f32
+                nu[x].astype(bf16), lift_weights, (((0,), (0,)), ((), ())), preferred_element_type=f32
             )
             val, slope = gelu_both(pre)
             slope1[x] = slope
@@ -97,13 +120,8 @@
             return c
 
         steps_of(8, lift, 0)
-        acc = None
-        for q in range(3):
-            for r in range(3):
-                lhs = vp[q : q + 8, r : r + 4].reshape(1024, 384)
-                d = jnp.dot(lhs, wf[q * 3 + r], preferred_element_type=f32)
-                acc = d if acc is None else acc + d
-        pre2[...] = acc
+        for x in range(8):
+            pre2[pl.ds(x * 128, 128), :] = conv_rows(vp, wf, x, 1)
 
         def out_step(x, c):
             loss, dwo = c
@@ -136,13 +154,8 @@
                     rows = pl.ds(((p * 3 + q) * 3 + r) * 128, 128)
                     piece = d[q * 128 : (q + 1) * 128, p * 128 : (p + 1) * 128]
                     conv_out[rows, :] += piece.astype(bf16).astype(f32)
-        acc = None
-        for q in range(3):
-            for r in range(3):
-                lhs = gp[2 - q : 10 - q, 2 - r : 6 - r].reshape(1024, 384)
-                d = jnp.dot(lhs, wb[q * 3 + r], preferred_element_type=f32)
-                acc = d if acc is None else acc + d
-        pre2[...] = acc
+        for x in range(8):
+            pre2[pl.ds(x * 128, 128), :] = conv_rows(gp, wb, x, -1)
 
         def back(x, c):
             dgain, dwl = c
@@ -162,11 +175,12 @@
         small_out[0:32, :] += dwl.astype(bf16).astype(f32)
         small_out[27:28, :] += dgain
         small_out[28:29, :] += dwo.astype(bf16).astype(f32)
-        small_out[32:33, :] += jnp.where(lane[0:1] == meta[1 + i, 0], 0.5 * loss, 0.0)
+        line = routed[pl.ds(META + 1 + i, 1), :]
+        small_out[32:33, :] += jnp.where(lane[0:1].astype(f32) == line, 0.5 * loss, 0.0)
         return carry
 
-    lax.fori_loop(0, meta[0, 0], patch, 0)
-    passed.wait()
+    number = jnp.max(routed[META : META + 1, :]).astype(jnp.int32)
+    lax.fori_loop(0, number, patch, 0)
 
 
 def lanes_of(shape):
@@ -220,7 +234,7 @@
 def route_kernel(
     n_gx, n_gy, n_ga,
     count, dest, start_x, start_y, field, prev_field, diffusivity, velocity,
-    new_field, batch, meta,
+    new_field, routed,
     state, later, prev, diff, speed, load_sem,
     mine, line, sent, group,
     z_in, x_out, x_in, y_out, y_in,
@@ -241,7 +255,7 @@
     ]
     for load in loads:
         load.start()
-    lane8 = lanes_of((8, 128))
+    sub8 = lax.broadcasted_iota(jnp.int32, (8, 128), 0)
     xi = lax.broadcasted_iota(jnp.int32, (size_x, 128), 0)
     li = lanes_of((size_x, 128))
     row_y = lax.broadcasted_iota(jnp.int32, (128, 128), 0)
@@ -422,21 +436,21 @@
                 for hit, old in zip(hits, picked)
             )
             origin = (source // 2) * n_gy + first_line + source % 2
-            lines = tuple(jnp.where(hit, origin, old) for hit, old in zip(hits, lines))
+            lines = tuple(jnp.where(hit, origin.astype(f32), old) for hit, old in zip(hits, lines))
         return base + number, picked, lines
 
-    none = jnp.zeros((8, 128), jnp.int32)
+    none = jnp.zeros((8, 128), f32)
     total, picked, lines = lax.fori_loop(
-        0, share, from_group, (jnp.zeros((8, 128), f32), (empty,) * CAP, (none,) * CAP)
+        0, share, from_group, (none, (empty,) * CAP, (none,) * CAP)
     )
     number = none
     for i in range(CAP):
-        batch[i] = picked[i].astype(bf16)
-        number = number + (place_f + share * i < total).astype(jnp.int32)
-    meta[0:1, :] = number[0:1]
+        routed[pl.ds(16 * i, 16), :] = picked[i]
+        number = number + (place_f + share * i < total).astype(f32)
+    rows = jnp.where(sub8 == 0, number, rank)
     for i in range(CAP):
-        meta[1 + i : 2 + i, :] = lines[i][0:1]
-    meta[5:8, :] = rank[0:3].astype(jnp.int32)
+        rows = jnp.where(sub8 == 1 + i, lines[i], rows)
+    routed[META : META + 8, :] = rows
 
     for copy in first + second + halos + more:
         copy.wait_send()
@@ -454,11 +468,10 @@
         functools.partial(route_kernel, n_gx, n_gy, n_ga),
         out_shape=(
             jax.ShapeDtypeStruct(field.shape, f32),
-            jax.ShapeDtypeStruct((CAP, 16, 128), bf16),
-            jax.ShapeDtypeStruct((8, 128), jnp.int32),
+            jax.ShapeDtypeStruct((META + 8, 128), f32),
         ),
         in_specs=[smem] * 4 + [hbm] * 4,
-        out_specs=(vmem,) * 3,
+        out_specs=(vmem,) * 2,
         scratch_shapes=[
             pltpu.VMEM((size_z + 2, size_x, size_y), f32),
             pltpu.VMEM((size_z + 2, size_x, size_y), f32),
@@ -488,21 +501,16 @@
     )(count, dest, start_x, start_y, field, prev_field, diffusivity, velocity)
 
 
-def train_call(meta, recs, w_lift, gain, w_conv, w_out, cells):
-    vm = pl.BlockSpec(memory_space=pltpu.VMEM)
-    hbm = pl.BlockSpec(memory_space=pltpu.HBM)
+def train_call(routed, w_lift, gain, w_conv, w_out):
+    vmem = pl.BlockSpec(memory_space=pltpu.VMEM)
     return pl.pallas_call(
         train_kernel,
-        out_shape=(
-            jax.ShapeDtypeStruct((3456, 128), f32),
-            jax.ShapeDtypeStruct((40, 128), f32),
-            jax.ShapeDtypeStruct(cells.shape, f32),
-        ),
-        in_specs=[pl.BlockSpec(memory_space=pltpu.SMEM)] + [vm] * 6,
-        out_specs=(vm, vm, hbm),
+        out_shape=(jax.ShapeDtypeStruct((3456, 128), f32), jax.ShapeDtypeStruct((40, 128), f32)),
+        in_specs=[vmem] * 5,
+        out_specs=(vmem, vmem),
         scratch_shapes=[
-            pltpu.VMEM((9, 384, 128), bf16),
-            pltpu.VMEM((9, 384, 128), bf16),
+            pltpu.VMEM((3, 384, 384), bf16),
+            pltpu.VMEM((3, 384, 384), bf16),
             pltpu.VMEM((10, 6, 32, 384), bf16),
             pltpu.VMEM((10, 6, 32, 384), bf16),
             pltpu.VMEM((10, 128, 128), bf16),
@@ -511,10 +519,10 @@
             pltpu.VMEM((8, 128, 128), f32),
             pltpu.VMEM((1024, 128), f32),
             pltpu.VMEM((8, 128, 128), bf16),
-            pltpu.SemaphoreType.DMA,
+            pltpu.VMEM((32, 128), f32),
         ],
         compiler_params=pltpu.CompilerParams(vmem_limit_bytes=32 * 1024 * 1024),
-    )(meta, recs, w_lift, gain, w_conv, w_out, cells)
+    )(routed, w_lift, gain, w_conv, w_out)
 
 
 def row_cuts(rows):
@@ -525,9 +533,9 @@
 
 def reduce_kernel(
     n_gx, n_gy, n_ga, rows, entries,
-    conv, small, meta,
+    conv, small, routed,
     total_out, tail_out,
-    ring, own, other, gathered, pieces, from_line, tile_b, from_group, tile_c, from_all,
+    leaf_out, leaf_in, ring, own, other, gathered, pieces, from_line, tile_b, from_group, tile_c, from_all,
     ring_send, ring_recv, pair_send, pair_recv, gather_send, gather_recv,
     a_send, a_recv, b_send, b_recv, c_send, c_recv,
 ):
@@ -566,14 +574,19 @@
     def ring_copy(step, side, part):
         low, size = subs[part]
         if step == 0:
-            src = conv.at[rows_of(gy + signs[side] * depth[side, part], part)]
-        else:
-            src = ring.at[step - 1, side, pl.ds(low, size)]
+            return remote(
+                leaf_out.at[side, pl.ds(low, size)], leaf_in.at[side, pl.ds(low, size)],
+                ring_send.at[0, side, part], ring_recv.at[0, side, part], next_to(side),
+            )
         return remote(
-            src, ring.at[step, side, pl.ds(low, size)],
+            ring.at[step - 1, side, pl.ds(low, size)], ring.at[step, side, pl.ds(low, size)],
             ring_send.at[step, side, part], ring_recv.at[step, side, part], next_to(side),
         )
 
+    for side, part in keys:
+        low, size = subs[part]
+        first = rows_of(gy + signs[side] * depth[side, part], part)
+        leaf_out[side, pl.ds(low, size), :] = conv[first, :].astype(bf16)
     started = []
 
     def begin(copy):
@@ -600,7 +613,9 @@
             flying[key].wait_recv()
             if step + 1 < depth[key]:
                 there = rows_of(gy + signs[side] * (depth[key] - 1 - step), part)
-                ring[step, side, pl.ds(low, size), :] += conv[there, :]
+                here = pl.ds(low, size)
+                came = leaf_in[side, here, :].astype(f32) if step == 0 else ring[step, side, here, :]
+                ring[step, side, here, :] = came + conv[there, :]
                 flying[key] = begin(ring_copy(step + 1, *key))
             elif step == far_side - 1:
                 here = pl.ds(low, size)
@@ -679,7 +694,7 @@
     )
     scale = lax.rsqrt(all_squares / entries + 1e-06)
     tail_out[0:32, :] = shared * scale
-    number = jnp.maximum(meta[5:6, :], 1).astype(f32)
+    number = jnp.maximum(routed[META + 5 : META + 6, :], 1.0)
     own_loss = jnp.sum(
         jnp.where(lane8[0:1] == line_id, summed[per + 1 : per + 2], 0.0), axis=1, keepdims=True
     )
@@ -689,7 +704,7 @@
         copy.wait_send()
 
 
-def reduce_call(conv, small, meta, entries):
+def reduce_call(conv, small, routed, entries):
     n_gx, n_gy, n_ga = (lax.axis_size(name) for name in ("gx", "gy", "ga"))
     share = n_gy * n_ga
     rows = conv.shape[0] // n_gy
@@ -704,6 +719,8 @@
         in_specs=[vmem] * 3,
         out_specs=(vmem,) * 2,
         scratch_shapes=[
+            pltpu.VMEM((2, rows, 128), bf16),
+            pltpu.VMEM((2, rows, 128), bf16),
             pltpu.VMEM((far_side, 2, rows, 128), f32),
             pltpu.VMEM((rows, 128), f32),
             pltpu.VMEM((rows, 128), f32),
@@ -724,7 +741,7 @@
         compiler_params=pltpu.CompilerParams(
             collective_id=1, has_side_effects=True, vmem_limit_bytes=32 * 1024 * 1024
         ),
-    )(conv, small, meta)
+    )(conv, small, routed)
 
 
 def finish_kernel(total, tail, conv_out, lift_out, gain_out, out_out, loss_out):
@@ -757,16 +774,13 @@
     field, prev_field, diffusivity, velocity, w_lift, norm_gain, w_conv, w_out,
     tile_count, patch_dest, anchor_x, anchor_y,
 ):
-    stepped, batch, meta = route_call(
+    new_field, routed = route_call(
         tile_count.reshape(1), patch_dest.reshape(2), anchor_x.reshape(2), anchor_y.reshape(2),
         field, prev_field, diffusivity, velocity,
     )
-    lift_rows = jnp.pad(w_lift, ((0, 32 - w_lift.shape[0]), (0, 0)))
-    conv, small, new_field = train_call(
-        meta, batch, lift_rows, norm_gain[None], w_conv[0], w_out[None], stepped
-    )
+    conv, small = train_call(routed, w_lift, norm_gain[None], w_conv[0], w_out[None])
     entries = w_lift.size + norm_gain.size + w_out.size + lax.axis_size("gx") * w_conv[0].size
-    total, tail = reduce_call(conv, small, meta, entries)
+    total, tail = reduce_call(conv, small, routed, entries)
     dir_conv, lift, gain, out, loss = finish_call(total, tail)
     return (
         new_field, loss[:, :1].reshape(1, 1, 1), lift, gain.reshape(-1),

time: 92.8 us -> 90.2 us (0.972)
  local copies, waits for them, and re-layouts: 3.15 us -> 1.58 us
    pallas_call x1, Pallas kernels: 14.7 us -> 11.3 us  [train_call(): pl.pallas_call(train_kernel, out_shape=(jax.ShapeDtypeStruct((3456, 128),...]
    pallas_call x1, Pallas kernels: 49.1 us -> 51.6 us  [reduce_call(): pl.pallas_call(functools.partial(reduce_kernel, n_gx, n_gy, n_ga, rows, e...]
    unnamed x12 -> x13, local copies, waits for them, and re-layouts: 2.45 us -> 1.58 us
where the time goes in v3:
time: 90.2 us; the launch traced here: 90.1 us
  Pallas kernels  87 us (96%)
  local copies, waits for them, and re-layouts  1.58 us (2%)
  between operations  1.45 us (2%)
    pallas_call x1, Pallas kernels, reduce_call(): pl.pallas_call(functools.partial(reduce_kernel, n_gx, n_gy, n_ga, rows, e...  51.6 us
    pallas_call x1, Pallas kernels, route_call(): pl.pallas_call(functools.partial(route_kernel, n_gx, n_gy, n_ga), out_sha...  22.9 us
    pallas_call x1, Pallas kernels, train_call(): pl.pallas_call(train_kernel, out_shape=(jax.ShapeDtypeStruct((3456, 128),...  11.3 us

profile of v3, /device:TPU:1, one launch (start us, length us, event | category | flops | bytes accessed | tf_op | source)
XLA Modules:
  0.0 90.1 jit_solution(11397243606707304863)
XLA Ops:
  0.6 0.0 copy-start.4
  0.6 0.0 copy-start
  0.7 0.0 copy-start.3
  0.7 0.0 copy-start.2
  1.4 22.9 %shard_map.163 = (f32[32,32,128]{2,1,0:T(8,128)}, f32[72,128]{1,0:T(8,128)}) custom-call(s32[1]{0:T(128)} %bitcast.12.count, s32[2]{0:T(128)} %bitcast.16, s32[2]{0:T(128)} %bitcast.17, s32[2]{0:T(128)} %bitcast.18, f32[32,32,128]{2,1,0:T(8,128)} %field.1, f32[32,32,128]{2,1,0:T(8,128)} %prev_field.1, f32[32,32,128]{2,1,0:T(8,128)} %diffusivity.1, ...), custom_call_target="tpu_custom_call" | custom-call | tf_op jit(solution)/shard_map/pallas_call | solution.py:467
  24.3 0.0 copy-done.4
  24.3 0.0 copy-done
  24.3 0.0 copy-done.3
  24.3 0.0 copy-done.2
  24.4 0.0 copy-start.1
  24.4 0.8 copy-done.1
  25.1 0.0 copy-start.5
  25.1 11.3 %shard_map.164 = (f32[3456,128]{1,0:T(8,128)S(1)}, f32[40,128]{1,0:T(8,128)S(1)}) custom-call(f32[72,128]{1,0:T(8,128)S(1)} %copy-done.1, bf16[27,128]{1,0:T(8,128)(2,1)S(1)} %copy-done.2, f32[1,128]{1,0:T(1,128)S(1)} %bitcast.14, bf16[3456,128]{1,0:T(8,128)(2,1)S(1)} %bitcast.13, bf16[1,128]{1,0:T(2,128)(2,1)S(1)} %bitcast.15), custom_call_target="tpu_custom_call" | custom-call | tf_op jit(solution)/shard_map/pallas_call | solution.py:506
  36.4 51.6 %shard_map.165 = (bf16[8,432,128]{2,1,0:T(8,128)(2,1)S(1)}, f32[40,128]{1,0:T(8,128)S(1)}) custom-call(f32[3456,128]{1,0:T(8,128)S(1)} %get-tuple-element.19.conv, f32[40,128]{1,0:T(8,128)S(1)} %get-tuple-element.20.small, f32[72,128]{1,0:T(8,128)S(1)} %copy-done.1), custom_call_target="tpu_custom_call" | custom-call | tf_op jit(solution)/shard_map/pallas_call | solution.py:714
  87.9 1.3 %shard_map.166 = (f32[3456,128]{1,0:T(8,128)}, f32[27,128]{1,0:T(8,128)}, f32[1,128]{1,0:T(1,128)}, f32[1,128]{1,0:T(1,128)}, f32[1,128]{1,0:T(1,128)}) custom-call(bf16[8,432,128]{2,1,0:T(8,128)(2,1)S(1)} %get-tuple-element.21.total, f32[40,128]{1,0:T(8,128)S(1)} %get-tuple-element.22.tail), custom_call_target="tpu_custom_call" | custom-call | tf_op jit(solution)/shard_map/pallas_call | solution.py:761
  89.3 0.0 copy-done.5
  89.3 0.8 copy.20
Async XLA Ops:
  0.6 23.7 %copy-start.4 = (bf16[128]{0:T(256)(128)(2,1)S(1)}, bf16[128]{0:T(256)(128)(2,1)}, u32[]{:S(2)}) copy-start(bf16[128]{0:T(256)(128)(2,1)} %param.19) | copy-start | bytes 772
  0.6 23.7 %copy-start = (bf16[1,3456,128]{2,1,0:T(8,128)(2,1)S(1)}, bf16[1,3456,128]{2,1,0:T(8,128)(2,1)}, u32[]{:S(2)}) copy-start(bf16[1,3456,128]{2,1,0:T(8,128)(2,1)} %param.18) | copy-start | bytes 2654212
  0.7 23.7 %copy-start.3 = (f32[128]{0:T(128)S(1)}, f32[128]{0:T(128)}, u32[]{:S(2)}) copy-start(f32[128]{0:T(128)} %param.17) | copy-start | bytes 1540
  0.7 23.7 %copy-start.2 = (bf16[27,128]{1,0:T(8,128)(2,1)S(1)}, bf16[27,128]{1,0:T(8,128)(2,1)}, u32[]{:S(2)}) copy-start(bf16[27,128]{1,0:T(8,128)(2,1)} %w_lift.1) | copy-start | bytes 20740
  24.4 0.8 copy-start.1
  25.1 64.2 %copy-start.5 = (f32[32,32,128]{2,1,0:T(8,128)S(1)}, f32[32,32,128]{2,1,0:T(8,128)}, u32[]{:S(2)}) copy-start(f32[32,32,128]{2,1,0:T(8,128)} %get-tuple-element.34) | copy-start | bytes 1572868

commit v4 on v3

v4 whole, which is shorter than its diff:
```python
import functools

import jax
import jax.numpy as jnp
from jax import lax
from jax.experimental import pallas as pl
from jax.experimental.pallas import tpu as pltpu
from jax.sharding import PartitionSpec as P

STEPS = 2
PVOX = 1024
CAP = 4
PAIR = 2
ROOT = 0.7978845608028654
CUBE = 0.044715
MESH = pl.DeviceIdType.MESH
f32, bf16 = jnp.float32, jnp.bfloat16


def gelu_both(v):
    v2 = v * v
    t = jnp.tanh(ROOT * (v + CUBE * (v * v2)))
    half = 0.5 * (1.0 + t)
    slope = half + 0.5 * v * (1.0 - t * t) * (ROOT * (1.0 + 3.0 * CUBE * v2))
    return v * half, slope


def z_shifted(block, z_ids):
    up = jnp.where(z_ids == 31, 0.0, pltpu.roll(block, 127, 0))
    down = jnp.where(z_ids == 0, 0.0, pltpu.roll(block, 1, 0))
    return up, down


def move_y(block, by):
    if by == 0:
        return block
    gap = jnp.zeros_like(block[:, :1])
    parts = [block[:, 1:], gap] if by > 0 else [gap, block[:, :-1]]
    return jnp.concatenate(parts, axis=1)


def conv_rows(source, weights, x, sign):
    acc = None
    number = source.shape[1]
    for q in range(3):
        x_in = x + sign * (q - 1)
        if x_in < 0 or x_in > 7:
            continue
        lhs = source[x_in + 1, :, 1:5].reshape(number * 128, 384)
        d = jnp.dot(lhs, weights[q], preferred_element_type=f32).reshape(number, 4, 32, 384)
        for r in range(3):
            piece = move_y(d[:, :, :, r * 128 : (r + 1) * 128], sign * (r - 1))
            acc = piece if acc is None else acc + piece
    return acc.reshape(number, 128, 128)


def lanes_of(shape):
    return lax.broadcasted_iota(jnp.int32, shape, len(shape) - 1)


def group_partners(n_gy, n_ga):
    gy, ga = lax.axis_index("gy"), lax.axis_index("ga")
    for far in range(1, n_gy * n_ga):
        there = (gy + far % n_gy) % n_gy
        across = (ga + far // n_gy) % n_ga
        yield far, {"gy": there, "ga": across}


def line_partners(n_gx):
    gx = lax.axis_index("gx")
    for far in range(1, n_gx):
        yield far, {"gx": (gx + far) % n_gx}


def meet(devices):
    barrier = pltpu.get_barrier_semaphore()
    for device in devices:
        pl.semaphore_signal(barrier, inc=1, device_id=device, device_id_type=MESH)
    return barrier, len(devices)


def several(count, step, carry, at_once=4):
    def run(block, carry):
        for i in range(at_once):
            carry = step(block * at_once + i, carry)
        return carry

    return lax.fori_loop(0, count // at_once, run, carry)


def remote(src, dst, send_sem, recv_sem, device):
    return pltpu.make_async_remote_copy(
        src_ref=src, dst_ref=dst, send_sem=send_sem, recv_sem=recv_sem,
        device_id=device, device_id_type=MESH,
    )


def row_cuts(rows):
    tiles = rows // 16
    ends = [16 * (tiles * i // 4 + (1 if 0 < i < 4 and tiles * i % 4 else 0)) for i in range(5)]
    return [(low, high - low) for low, high in zip(ends, ends[1:])]


def whole_kernel(
    n_gx, n_gy, n_ga, rows, entries,
    count, dest, start_x, start_y, field, prev_field, diffusivity, velocity,
    w_lift, gain, w_conv, w_out,
    new_field, total_out, tail_out, *scratch,
):
    (
        state, later, prev, diff, speed, weights,
        mine, line, z_in, x_out, x_in, y_out, y_in, records,
        wf, wb, lift_rows, vp, gp, nt, nu, lifted, slope1, pre2, dh,
        conv, small, leaf_out, leaf_in, ring, own, other, gathered,
        pieces, from_line_sums, tile_b, from_group, tile_c, from_all,
        load_sem, line_send, line_recv, halo_send, halo_recv,
        ring_send, ring_recv, pair_send, pair_recv, gather_send, gather_recv,
        a_send, a_recv, b_send, b_recv, c_send, c_recv,
    ) = scratch
    gx, gy, ga = lax.axis_index("gx"), lax.axis_index("gy"), lax.axis_index("ga")
    line_id = ga * n_gy + gy
    barrier, expected = meet(
        [device for _, device in line_partners(n_gx)]
        + [device for _, device in group_partners(n_gy, n_ga)]
    )
    size_z, size_x, size_y = prev.shape
    loads = [
        pltpu.make_async_copy(field, state.at[pl.ds(1, size_z)], load_sem.at[0]),
        pltpu.make_async_copy(prev_field, prev, load_sem.at[1]),
        pltpu.make_async_copy(diffusivity, diff, load_sem.at[2]),
        pltpu.make_async_copy(velocity, speed, load_sem.at[3]),
        pltpu.make_async_copy(w_conv, weights, load_sem.at[4]),
    ]
    for load in loads:
        load.start()
    sub8 = lax.broadcasted_iota(jnp.int32, (8, 128), 0)
    lane8 = lanes_of((8, 128))
    xi = lax.broadcasted_iota(jnp.int32, (size_x, 128), 0)
    li = lanes_of((size_x, 128))
    row_y = lax.broadcasted_iota(jnp.int32, (128, 128), 0)
    col = lanes_of((128, 128))
    z_mask = (
        lax.broadcasted_iota(jnp.int32, (size_z, 8, 128), 0) == lanes_of((size_z, 8, 128)) % size_z
    )
    zero_tile = jnp.zeros((size_x, 128), f32)
    for held in (vp, gp, nt, nu, lifted, slope1, dh, conv, small, lift_rows):
        held[...] = jnp.zeros_like(held)
    lift_rows[0:27, :] = w_lift[...].astype(f32)
    lift_weights = lift_rows[...].astype(bf16)
    gain_row = gain[...]
    wo_row = w_out[...].astype(f32)

    def pack_faces(step, cells, high, low):
        x_out[step, 0] = cells[1 : size_z + 1, 0, :]
        x_out[step, 1] = cells[1 : size_z + 1, size_x - 1, :]
        y_out[step, 0] = low
        y_out[step, 1] = high

    def halo_copies(step, cells):
        base = step * 5
        z_src = cells.at[size_z - (size_z - 1) * ga]
        there = {"ga": 1 - ga}
        z_out_copy = remote(
            z_src, z_in.at[step], halo_send.at[base], halo_recv.at[base], there
        )
        copies = [z_out_copy]
        for side in range(2):
            near = (gx + (n_gx - 1 if side == 0 else 1)) % n_gx
            copies.append(remote(
                x_out.at[step, side], x_in.at[step, 1 - side],
                halo_send.at[base + 1 + side], halo_recv.at[base + 1 + side], {"gx": near},
            ))
        for side in range(2):
            near = (gy + (n_gy - 1 if side == 0 else 1)) % n_gy
            copies.append(remote(
                y_out.at[step, side], y_in.at[step, 1 - side],
                halo_send.at[base + 3 + side], halo_recv.at[base + 3 + side], {"gy": near},
            ))
        return copies

    def place(z, cells, high, low):
        high = jnp.where(li == z, pltpu.roll(cells, z + 1, 1), high)
        low = jnp.where(li == z, pltpu.roll(cells, z, 1), low)
        return high, low

    def advance(step, cells, store, pack):
        z_face = z_in[step]
        cells[0] = jnp.where(ga == 1, z_face, 0.0)
        cells[size_z + 1] = jnp.where(ga == 0, z_face, 0.0)

        def layer(z, faces):
            centre = cells[z + 1]
            below = cells[z]
            above = cells[z + 2]
            behind = jnp.where(xi == 0, x_in[step, 0, pl.ds(z, 1), :], pltpu.roll(centre, 1, 0))
            ahead = jnp.where(
                xi == size_x - 1, x_in[step, 1, pl.ds(z, 1), :], pltpu.roll(centre, size_x - 1, 0)
            )
            left = jnp.where(
                li == 0, pltpu.roll(y_in[step, 0], 128 - z, 1), pltpu.roll(centre, 1, 1)
            )
            right = jnp.where(
                li == 127, pltpu.roll(y_in[step, 1], 127 - z, 1), pltpu.roll(centre, 127, 1)
            )
            laplace = above + below + (ahead + behind) + (right + left) - 6.0 * centre
            moved = jnp.zeros_like(centre)
            for d, (low, high) in enumerate(((below, above), (behind, ahead), (left, right))):
                v = speed[d, z]
                moved = moved + (
                    jnp.maximum(v, 0.0) * (centre - low) + jnp.minimum(v, 0.0) * (high - centre)
                )
            result = centre + diff[z] * laplace - moved
            store(z, result)
            return place(z, result, *faces) if pack else faces

        return several(size_z, layer, (zero_tile, zero_tile))

    loads[0].wait()
    high, low = several(
        size_z, lambda z, faces: place(z, state[z + 1], *faces), (zero_tile, zero_tile)
    )
    pack_faces(0, state, high, low)
    loads[1].wait()
    for k in range(2):
        chosen = (row_y == start_y[k] + col // size_z).astype(bf16)
        parts = []
        for source in (0, 1):
            if source == 0:
                window = prev[:, pl.ds(start_x[k], 8), :]
            else:
                window = state[1 : size_z + 1, pl.ds(start_x[k], 8), :]
            spread = jnp.dot(
                window.reshape(size_z * 8, 128).astype(bf16), chosen, preferred_element_type=f32
            ).reshape(size_z, 8, 128)
            parts.append(jnp.sum(jnp.where(z_mask, spread, 0.0), axis=0))
        mine[pl.ds(16 * k, 16), :] = jnp.concatenate(parts, axis=0).astype(bf16)
    goals = [jnp.where(k < count[0], dest[k], -1).astype(f32) for k in range(2)]
    mine[32:48, :] = jnp.concatenate(
        [jnp.full((8, 128), goals[0]), jnp.full((8, 128), goals[1])], axis=0
    ).astype(bf16)
    line[gx] = mine[...]

    pl.semaphore_wait(barrier, expected)
    first = []
    for far, device in line_partners(n_gx):
        copy = remote(mine, line.at[gx], line_send.at[far], line_recv.at[far], device)
        copy.start()
        first.append(copy)
    halos = halo_copies(0, state)
    for copy in halos:
        copy.start()

    loads[4].wait()
    for q in range(3):
        for r in range(3):
            for p in range(3):
                blk = weights[pl.ds(((p * 3 + q) * 3 + r) * 128, 128), :]
                wf[q, pl.ds(p * 128, 128), pl.ds(r * 128, 128)] = blk
                wb[q, pl.ds(p * 128, 128), pl.ds(r * 128, 128)] = blk.astype(f32).T.astype(bf16)

    loads[2].wait()
    loads[3].wait()
    for copy in halos:
        copy.wait_recv()

    def keep(z, value):
        later[z + 1] = value

    high, low = advance(0, state, keep, True)
    pack_faces(1, later, high, low)
    more = halo_copies(1, later)
    for copy in more:
        copy.start()

    for copy in first:
        copy.wait_recv()
    empty = jnp.zeros((16, 128), f32)
    myself = gx.astype(f32)

    def from_line(source, carry):
        rank, picked = carry
        for k in range(2):
            goal = line[source, 32:48, :].astype(f32)[8 * k : 8 * k + 8]
            record = line[source, pl.ds(16 * k, 16), :].astype(f32)
            hit = goal == myself
            picked = tuple(
                jnp.where(jnp.concatenate([hit & (rank == c)] * 2, axis=0), record, old)
                for c, old in enumerate(picked)
            )
            rank = rank + hit.astype(f32)
        return rank, picked

    rank, picked = lax.fori_loop(
        0, n_gx, from_line, (jnp.zeros((8, 128), f32), (empty,) * CAP)
    )
    for c in range(CAP):
        records[pl.ds(16 * c, 16), :] = picked[c]

    z_ids = lax.broadcasted_iota(jnp.int32, (128, 128), 0) % 32

    def first_part(i):
        for slot in range(PAIR):
            u = records[pl.ds(16 * (PAIR * i + slot), 8), :]
            for p in range(3):
                dz = p - 1
                uz = u if dz == 0 else pltpu.roll(u, (-dz) % 128, 1)
                okz = (lane8 % 32 + dz >= 0) & (lane8 % 32 + dz < 32)
                for q in range(3):
                    dx = q - 1
                    ux = uz if dx == 0 else pltpu.roll(uz, (-dx) % 8, 0)
                    okx = (sub8 + dx >= 0) & (sub8 + dx < 8)
                    for r in range(3):
                        dy = r - 1
                        uy = ux if dy == 0 else pltpu.roll(ux, (-32 * dy) % 128, 1)
                        oky = (lane8 // 32 + dy >= 0) & (lane8 // 32 + dy < 4)
                        nu[slot, :, p * 9 + q * 3 + r, :] = jnp.where(okz & okx & oky, uy, 0.0)
            for x in range(8):
                pre = lax.dot_general(
                    nu[slot, x].astype(bf16), lift_weights, (((0,), (0,)), ((), ())), preferred_element_type=f32
                )
                val, slope = gelu_both(pre)
                slope1[slot, x] = slope
                low = val.astype(bf16)
                lifted[slot, x] = low
                wide = low.astype(f32)
                inv = lax.rsqrt(jnp.mean(wide * wide, axis=1, keepdims=True) + 1e-06)
                normed = (wide * inv * gain_row).astype(bf16).astype(f32)
                up, down = z_shifted(normed, z_ids)
                for k, v in enumerate((down, normed, up)):
                    vp[x + 1, slot, 1:5, :, k * 128 : (k + 1) * 128] = v.astype(bf16).reshape(4, 32, 128)
                nt[slot, x + 1] = normed.T.astype(bf16)
        for x in range(8):
            pre2[x] = conv_rows(vp, wf, x, 1)
        for slot in range(PAIR):
            target = records[pl.ds(16 * (PAIR * i + slot) + 8, 8), :]
            loss = dwo = jnp.zeros((1, 128), f32)
            for x in range(8):
                mixed, slope = gelu_both(pre2[x, slot])
                hid = (lifted[slot, x].astype(f32) + mixed).astype(bf16).astype(f32)
                pred = jnp.sum(hid * wo_row, axis=1, keepdims=True)
                row = jnp.sum(jnp.where(sub8 == x, target, 0.0), axis=0, keepdims=True)
                wanted = jnp.broadcast_to(row, (128, 128)).T
                misfit = pred - wanted
                loss = loss + jnp.sum(misfit * misfit, axis=0, keepdims=True)
                dwo = dwo + jnp.sum(hid * misfit, axis=0, keepdims=True)
                d_hid = (misfit * wo_row).astype(bf16)
                dh[slot, x] = d_hid
                g = (d_hid.astype(f32) * slope).astype(bf16).astype(f32)
                up, down = z_shifted(g, z_ids)
                for k, v in enumerate((up, g, down)):
                    gp[x + 1, slot, 1:5, :, k * 128 : (k + 1) * 128] = v.astype(bf16).reshape(4, 32, 128)
            lhs = jnp.concatenate(
                [jnp.concatenate([nt[slot, q + x] for x in range(8)], axis=1) for q in range(3)], axis=0
            )
            for r in range(3):
                rhs = gp[1:9, slot, 2 - r : 6 - r].reshape(1024, 384)
                d = jnp.dot(lhs, rhs, preferred_element_type=f32)
                for q in range(3):
                    for p in range(3):
                        rows = pl.ds(((p * 3 + q) * 3 + r) * 128, 128)
                        piece = d[q * 128 : (q + 1) * 128, p * 128 : (p + 1) * 128]
                        conv[rows, :] += piece.astype(bf16).astype(f32)
            small[28:29, :] += dwo.astype(bf16).astype(f32)
            small[32:33, :] += 0.5 * loss

    def second_part():
        for x in range(8):
            pre2[x] = conv_rows(gp, wb, x, -1)
        for slot in range(PAIR):
            dgain, dwl = jnp.zeros((1, 128), f32), jnp.zeros((32, 128), f32)
            for x in range(8):
                dn = pre2[x, slot].astype(bf16).astype(f32)
                wide = lifted[slot, x].astype(f32)
                inv = lax.rsqrt(jnp.mean(wide * wide, axis=1, keepdims=True) + 1e-06)
                unit = wide * inv
                dgain = dgain + jnp.sum(dn * unit, axis=0, keepdims=True)
                dt = dn * gain_row
                mean = jnp.sum(dt * wide, axis=1, keepdims=True) * (1.0 / 128.0)
                d_low = dh[slot, x].astype(f32) + dt * inv - (inv * inv * inv * mean) * wide
                d_pre = d_low.astype(bf16).astype(f32) * slope1[slot, x]
                dwl = dwl + jnp.dot(nu[slot, x].astype(bf16), d_pre.astype(bf16), preferred_element_type=f32)
            small[0:32, :] += dwl.astype(bf16).astype(f32)
            small[27:28, :] += dgain

    def one_pair(i, carry):
        pl.when(i > 0)(second_part)
        first_part(i)
        return carry

    lax.fori_loop(0, CAP // PAIR, one_pair, 0)

    subs = row_cuts(rows)
    far_side = n_gy // 2
    signs = (1, -1)
    keys = [(0, 0), (1, 2), (0, 1), (1, 3), (0, 2), (1, 0), (0, 3), (1, 1)]
    depth = {(side, part): far_side if part // 2 == side else n_gy - 1 - far_side for side, part in keys}
    share = n_gy * n_ga
    per = 32 // n_gx

    def wrap(index):
        return (index + 2 * n_gy) % n_gy

    def rows_of(index, part):
        low, size = subs[part]
        return pl.ds(pl.multiple_of(wrap(index) * rows + low, 8), size)

    def next_to(side):
        return {"gy": wrap(gy + signs[side])}

    def ring_copy(step, side, part):
        low, size = subs[part]
        if step == 0:
            return remote(
                leaf_out.at[side, pl.ds(low, size)], leaf_in.at[side, pl.ds(low, size)],
                ring_send.at[0, side, part], ring_recv.at[0, side, part], next_to(side),
            )
        return remote(
            ring.at[step - 1, side, pl.ds(low, size)], ring.at[step, side, pl.ds(low, size)],
            ring_send.at[step, side, part], ring_recv.at[step, side, part], next_to(side),
        )

    for side, part in keys:
        low, size = subs[part]
        leaf = rows_of(gy + signs[side] * depth[side, part], part)
        leaf_out[side, pl.ds(low, size), :] = conv[leaf, :].astype(bf16)
    started = []

    def begin(copy):
        copy.start()
        started.append(copy)
        return copy

    flying = {key: begin(ring_copy(0, *key)) for key in keys}
    second_part()

    for k in range(n_gx):
        pieces[k] = jnp.concatenate(
            [small[per * k : per * k + per, :], jnp.zeros((8 - per, 128), f32)], axis=0
        )
    from_line_sums[gx] = pieces[gx]

    line_copies = [
        begin(remote(
            pieces.at[device["gx"]], from_line_sums.at[gx], a_send.at[far], a_recv.at[far], device
        ))
        for far, device in line_partners(n_gx)
    ]

    pairs = {}
    for step in range(far_side):
        for key in keys:
            side, part = key
            low, size = subs[part]
            if step >= depth[key]:
                continue
            flying[key].wait_recv()
            if step + 1 < depth[key]:
                there = rows_of(gy + signs[side] * (depth[key] - 1 - step), part)
                here = pl.ds(low, size)
                came = leaf_in[side, here, :].astype(f32) if step == 0 else ring[step, side, here, :]
                ring[step, side, here, :] = came + conv[there, :]
                flying[key] = begin(ring_copy(step + 1, *key))
            elif step == far_side - 1:
                here = pl.ds(low, size)
                near = depth[1 - side, part] - 1
                own[here, :] = (
                    ring[step, side, here, :] + ring[near, 1 - side, here, :]
                ) + conv[rows_of(gy, part), :]
                pairs[part] = begin(remote(
                    own.at[here], other.at[here], pair_send.at[part], pair_recv.at[part],
                    {"ga": 1 - ga},
                ))

    for copy in line_copies:
        copy.wait_recv()
    piece = lax.fori_loop(0, n_gx, lambda k, acc: acc + from_line_sums[k], jnp.zeros((8, 128), f32))

    def gather_copy(step, side, part):
        low, size = subs[part]
        where = gathered.at[wrap(gy - signs[side] * step), pl.ds(low, size)]
        return remote(
            where, where,
            gather_send.at[step, side, part], gather_recv.at[step, side, part], next_to(side),
        )

    squares = jnp.zeros((1, 128), f32)
    for part in (0, 2, 1, 3):
        low, size = subs[part]
        here = pl.ds(low, size)
        pairs[part].wait_recv()
        total = own[here, :] + other[here, :]
        gathered[gy, here, :] = total.astype(bf16)
        for side in (part // 2, 1 - part // 2):
            flying[side, part] = begin(gather_copy(0, side, part))
        squares = squares + jnp.sum(total * total, axis=0, keepdims=True)
    squares = jnp.where(ga == 0, squares, 0.0)
    tile_b[...] = jnp.where(sub8 < per, piece, jnp.where(sub8 == per, squares, 0.0))
    from_group[line_id] = tile_b[...]
    group_copies = [
        begin(remote(tile_b, from_group.at[line_id], b_send.at[far], b_recv.at[far], device))
        for far, device in group_partners(n_gy, n_ga)
    ]

    for copy in more:
        copy.wait_recv()

    def emit(z, value):
        new_field[z] = value

    advance(1, later, emit, False)
    for step in range(far_side):
        for key in keys:
            if step >= depth[key]:
                continue
            flying[key].wait_recv()
            if step + 1 < depth[key]:
                flying[key] = begin(gather_copy(step + 1, *key))
        if step == 1:
            for copy in group_copies:
                copy.wait_recv()
            summed = lax.fori_loop(
                0, share, lambda k, acc: acc + from_group[k], jnp.zeros((8, 128), f32)
            )
            tile_c[...] = summed
            from_all[gx] = summed
            last_copies = [
                begin(remote(tile_c, from_all.at[gx], c_send.at[far], c_recv.at[far], device))
                for far, device in line_partners(n_gx)
            ]

    total_out[...] = gathered[...]
    for copy in last_copies:
        copy.wait_recv()
    shared = jnp.concatenate([from_all[k, 0:per, :] for k in range(n_gx)], axis=0)
    conv_squares = lax.fori_loop(
        0, n_gx, lambda k, acc: acc + from_all[k], jnp.zeros((8, 128), f32)
    )[per : per + 1]
    all_squares = jnp.sum(
        conv_squares + jnp.sum(shared * shared, axis=0, keepdims=True), axis=1, keepdims=True
    )
    scale = lax.rsqrt(all_squares / entries + 1e-06)
    tail_out[0:32, :] = shared * scale
    loss = small[32:33, :] / (PVOX * jnp.maximum(rank[0:1], 1.0))
    tail_out[32:40, :] = jnp.where(sub8 == 0, jnp.broadcast_to(scale, (8, 128)), loss)
    for copy in started + first + halos + more:
        copy.wait_send()


def whole_call(
    count, dest, start_x, start_y, field, prev_field, diffusivity, velocity,
    w_lift, gain, w_conv, w_out, entries,
):
    n_gx, n_gy, n_ga = (lax.axis_size(name) for name in ("gx", "gy", "ga"))
    size_z, size_x, size_y = field.shape
    share = n_gy * n_ga
    rows = w_conv.shape[0] // n_gy
    far_side = n_gy // 2
    smem = pl.BlockSpec(memory_space=pltpu.SMEM)
    vmem = pl.BlockSpec(memory_space=pltpu.VMEM)
    hbm = pl.BlockSpec(memory_space=pl.ANY)
    dma = pltpu.SemaphoreType.DMA
    held = pltpu.VMEM
    return pl.pallas_call(
        functools.partial(whole_kernel, n_gx, n_gy, n_ga, rows, entries),
        out_shape=(
            jax.ShapeDtypeStruct(field.shape, f32),
            jax.ShapeDtypeStruct((n_gy, rows, 128), bf16),
            jax.ShapeDtypeStruct((40, 128), f32),
        ),
        in_specs=[smem] * 4 + [hbm] * 4 + [vmem, vmem, hbm, vmem],
        out_specs=(vmem,) * 3,
        scratch_shapes=[
            held((size_z + 2, size_x, size_y), f32),
            held((size_z + 2, size_x, size_y), f32),
            held((size_z, size_x, size_y), f32),
            held((size_z, size_x, size_y), f32),
            held((3, size_z, size_x, size_y), f32),
            held(w_conv.shape, bf16),
            held((48, 128), bf16),
            held((n_gx, 48, 128), bf16),
            held((STEPS, size_x, 128), f32),
            held((STEPS, 2, size_z, 128), f32),
            held((STEPS, 2, size_z, 128), f32),
            held((STEPS, 2, size_x, 128), f32),
            held((STEPS, 2, size_x, 128), f32),
            held((16 * CAP, 128), f32),
            held((3, 384, 384), bf16),
            held((3, 384, 384), bf16),
            held((32, 128), f32),
            held((10, PAIR, 6, 32, 384), bf16),
            held((10, PAIR, 6, 32, 384), bf16),
            held((PAIR, 10, 128, 128), bf16),
            held((PAIR, 8, 32, 128), f32),
            held((PAIR, 8, 128, 128), bf16),
            held((PAIR, 8, 128, 128), f32),
            held((8, PAIR, 128, 128), f32),
            held((PAIR, 8, 128, 128), bf16),
            held(w_conv.shape, f32),
            held((40, 128), f32),
            held((2, rows, 128), bf16),
            held((2, rows, 128), bf16),
            held((far_side, 2, rows, 128), f32),
            held((rows, 128), f32),
            held((rows, 128), f32),
            held((n_gy, rows, 128), bf16),
            held((n_gx, 8, 128), f32),
            held((n_gx, 8, 128), f32),
            held((8, 128), f32),
            held((share, 8, 128), f32),
            held((8, 128), f32),
            held((n_gx, 8, 128), f32),
            dma((5,)),
            dma((n_gx,)), dma((n_gx,)),
            dma((STEPS * 5,)), dma((STEPS * 5,)),
            dma((far_side, 2, 4)), dma((far_side, 2, 4)),
            dma((4,)), dma((4,)),
            dma((far_side, 2, 4)), dma((far_side, 2, 4)),
            dma((n_gx,)), dma((n_gx,)),
            dma((share,)), dma((share,)),
            dma((n_gx,)), dma((n_gx,)),
        ],
        compiler_params=pltpu.CompilerParams(
            collective_id=0, has_side_effects=True, vmem_limit_bytes=56 * 1024 * 1024
        ),
    )(
        count, dest, start_x, start_y, field, prev_field, diffusivity, velocity,
        w_lift, gain, w_conv, w_out,
    )


def finish_kernel(total, tail, cells, conv_out, lift_out, gain_out, out_out, loss_out, cells_out):
    cells_out[...] = cells[...]
    scale = tail[32:33, :]
    for chunk in range(total.shape[0]):
        size = total.shape[1]
        conv_out[pl.ds(chunk * size, size), :] = total[chunk].astype(f32) * scale
    lift_out[...] = tail[0:27, :]
    gain_out[...] = tail[27:28, :]
    out_out[...] = tail[28:29, :]
    loss_out[...] = tail[33:34, :]


def finish_call(total, tail, cells):
    vmem = pl.BlockSpec(memory_space=pltpu.VMEM)
    tile = functools.partial(jax.ShapeDtypeStruct, dtype=f32)
    return pl.pallas_call(
        finish_kernel,
        out_shape=(
            tile((total.shape[0] * total.shape[1], 128)),
            tile((27, 128)), tile((1, 128)), tile((1, 128)), tile((1, 128)),
            tile(cells.shape),
        ),
        in_specs=[vmem] * 3,
        out_specs=(vmem,) * 6,
        compiler_params=pltpu.CompilerParams(vmem_limit_bytes=56 * 1024 * 1024),
    )(total, tail, cells)


def body(
    field, prev_field, diffusivity, velocity, w_lift, norm_gain, w_conv, w_out,
    tile_count, patch_dest, anchor_x, anchor_y,
):
    entries = w_lift.size + norm_gain.size + w_out.size + lax.axis_size("gx") * w_conv[0].size
    stepped, total, tail = whole_call(
        tile_count.reshape(1), patch_dest.reshape(2), anchor_x.reshape(2), anchor_y.reshape(2),
        field, prev_field, diffusivity, velocity,
        w_lift, norm_gain[None], w_conv[0], w_out[None], entries,
    )
    dir_conv, lift, gain, out, loss, new_field = finish_call(total, tail, stepped)
    return (
        new_field, loss[:, :1].reshape(1, 1, 1), lift, gain.reshape(-1),
        dir_conv.reshape(w_conv.shape), out.reshape(-1),
    )


def solution(mesh):
    tiles = P("ga", "gx", "gy")
    slots = P("ga", "gx", "gy", None)
    in_specs = (
        tiles, tiles, tiles, P(None, "ga", "gx", "gy"), P(), P(), P("gx", None, None), P(),
        tiles, slots, slots, slots,
    )
    out_specs = (tiles, tiles, P(), P(), P("gx", None, None), P())
    return jax.shard_map(body, mesh=mesh, in_specs=in_specs, out_specs=out_specs, check_vma=False)
```

time: 90.2 us -> 79.5 us (0.88)
  Pallas kernels: 87 us -> 78.1 us
  local copies, waits for them, and re-layouts: 1.58 us -> 0 us
    pallas_call x3 -> x1, Pallas kernels: 85.7 us -> 75.3 us  [whole_call(): pl.pallas_call(functools.partial(whole_kernel, n_gx, n_gy, n_ga, rows, en...]
    unnamed x13 -> x0, local copies, waits for them, and re-layouts: 1.58 us -> none
    pallas_call x1, Pallas kernels: 1.33 us -> 2.8 us  [finish_call(): pl.pallas_call(finish_kernel, out_shape=(tile((total.shape[0] * total.sha...]
where the time goes in v4:
time: 79.5 us; the launch traced here: 79.4 us
  Pallas kernels  78.1 us (98%)
  between operations  1.29 us (2%)
    pallas_call x1, Pallas kernels, whole_call(): pl.pallas_call(functools.partial(whole_kernel, n_gx, n_gy, n_ga, rows, en...  75.3 us
    pallas_call x1, Pallas kernels, finish_call(): pl.pallas_call(finish_kernel, out_shape=(tile((total.shape[0] * total.sha...  2.8 us

profile of v4, /device:TPU:1, one launch (start us, length us, event | category | flops | bytes accessed | tf_op | source)
XLA Modules:
  0.0 79.4 jit_solution(8868806151029970181)
XLA Ops:
  1.3 75.3 %shard_map.163 = (f32[32,32,128]{2,1,0:T(8,128)}, bf16[8,432,128]{2,1,0:T(8,128)(2,1)}, f32[40,128]{1,0:T(8,128)}) custom-call(s32[1]{0:T(128)} %bitcast.12.count, s32[2]{0:T(128)} %bitcast.14, s32[2]{0:T(128)} %bitcast.15, s32[2]{0:T(128)} %bitcast.16, f32[32,32,128]{2,1,0:T(8,128)} %field.1, f32[32,32,128]{2,1,0:T(8,128)} %prev_field.1, ...), custom_call_target="tpu_custom_call" | custom-call | tf_op jit(solution)/shard_map/pallas_call | solution.py:563
  76.5 2.8 %shard_map.164 = (f32[3456,128]{1,0:T(8,128)}, f32[27,128]{1,0:T(8,128)}, f32[1,128]{1,0:T(1,128)}, f32[1,128]{1,0:T(1,128)}, f32[1,128]{1,0:T(1,128)}, /*index=5*/f32[32,32,128]{2,1,0:T(8,128)}) custom-call(bf16[8,432,128]{2,1,0:T(8,128)(2,1)} %get-tuple-element.15.total, f32[40,128]{1,0:T(8,128)} %get-tuple-element.16.tail, ...), custom_call_target="tpu_custom_call" | custom-call | tf_op jit(solution)/shard_map/pallas_call | solution.py:646

commit v5 on v4

--- a/solution.py
+++ b/solution.py
@@ -11,6 +11,7 @@
 PVOX = 1024
 CAP = 4
 PAIR = 2
+BEFORE = 5
 ROOT = 0.7978845608028654
 CUBE = 0.044715
 MESH = pl.DeviceIdType.MESH
@@ -41,7 +42,7 @@
 
 def conv_rows(source, weights, x, sign):
     acc = None
-    number = source.shape[1]
+    number = PAIR
     for q in range(3):
         x_in = x + sign * (q - 1)
         if x_in < 0 or x_in > 7:
@@ -103,7 +104,7 @@
 
 def whole_kernel(
     n_gx, n_gy, n_ga, rows, entries,
-    count, dest, start_x, start_y, field, prev_field, diffusivity, velocity,
+    count_in, dest_in, start_x_in, start_y_in, field, prev_field, diffusivity, velocity,
     w_lift, gain, w_conv, w_out,
     new_field, total_out, tail_out, *scratch,
 ):
@@ -116,13 +117,10 @@
         load_sem, line_send, line_recv, halo_send, halo_recv,
         ring_send, ring_recv, pair_send, pair_recv, gather_send, gather_recv,
         a_send, a_recv, b_send, b_recv, c_send, c_recv,
+        count, dest, start_x, start_y,
     ) = scratch
     gx, gy, ga = lax.axis_index("gx"), lax.axis_index("gy"), lax.axis_index("ga")
     line_id = ga * n_gy + gy
-    barrier, expected = meet(
-        [device for _, device in line_partners(n_gx)]
-        + [device for _, device in group_partners(n_gy, n_ga)]
-    )
     size_z, size_x, size_y = prev.shape
     loads = [
         pltpu.make_async_copy(field, state.at[pl.ds(1, size_z)], load_sem.at[0]),
@@ -131,8 +129,18 @@
         pltpu.make_async_copy(velocity, speed, load_sem.at[3]),
         pltpu.make_async_copy(w_conv, weights, load_sem.at[4]),
     ]
+    loads += [
+        pltpu.make_async_copy(source, held, load_sem.at[5 + i])
+        for i, (source, held) in enumerate(
+            ((count_in, count), (dest_in, dest), (start_x_in, start_x), (start_y_in, start_y))
+        )
+    ]
     for load in loads:
         load.start()
+    barrier, expected = meet(
+        [device for _, device in line_partners(n_gx)]
+        + [device for _, device in group_partners(n_gy, n_ga)]
+    )
     sub8 = lax.broadcasted_iota(jnp.int32, (8, 128), 0)
     lane8 = lanes_of((8, 128))
     xi = lax.broadcasted_iota(jnp.int32, (size_x, 128), 0)
@@ -143,12 +151,6 @@
         lax.broadcasted_iota(jnp.int32, (size_z, 8, 128), 0) == lanes_of((size_z, 8, 128)) % size_z
     )
     zero_tile = jnp.zeros((size_x, 128), f32)
-    for held in (vp, gp, nt, nu, lifted, slope1, dh, conv, small, lift_rows):
-        held[...] = jnp.zeros_like(held)
-    lift_rows[0:27, :] = w_lift[...].astype(f32)
-    lift_weights = lift_rows[...].astype(bf16)
-    gain_row = gain[...]
-    wo_row = w_out[...].astype(f32)
 
     def pack_faces(step, cells, high, low):
         x_out[step, 0] = cells[1 : size_z + 1, 0, :]
@@ -221,6 +223,8 @@
     )
     pack_faces(0, state, high, low)
     loads[1].wait()
+    for load in loads[5:]:
+        load.wait()
     for k in range(2):
         chosen = (row_y == start_y[k] + col // size_z).astype(bf16)
         parts = []
@@ -250,6 +254,17 @@
     for copy in halos:
         copy.start()
 
+    for held in (nu, conv, small, lift_rows):
+        held[...] = jnp.zeros_like(held)
+    for edge in (0, 5):
+        gp[:, :, :, edge] = jnp.zeros_like(gp[:, :, :, edge])
+    for edge in (0, 9):
+        nt[:, edge] = jnp.zeros_like(nt[:, edge])
+    lift_rows[0:27, :] = w_lift[...].astype(f32)
+    lift_weights = lift_rows[...].astype(bf16)
+    gain_row = gain[...]
+    wo_row = w_out[...].astype(f32)
+
     loads[4].wait()
     for q in range(3):
         for r in range(3):
@@ -313,15 +328,15 @@
                         dy = r - 1
                         uy = ux if dy == 0 else pltpu.roll(ux, (-32 * dy) % 128, 1)
                         oky = (lane8 // 32 + dy >= 0) & (lane8 // 32 + dy < 4)
-                        nu[slot, :, p * 9 + q * 3 + r, :] = jnp.where(okz & okx & oky, uy, 0.0)
+                        nu[i, slot, :, p * 9 + q * 3 + r, :] = jnp.where(okz & okx & oky, uy, 0.0)
             for x in range(8):
                 pre = lax.dot_general(
-                    nu[slot, x].astype(bf16), lift_weights, (((0,), (0,)), ((), ())), preferred_element_type=f32
+                    nu[i, slot, x].astype(bf16), lift_weights, (((0,), (0,)), ((), ())), preferred_element_type=f32
                 )
                 val, slope = gelu_both(pre)
-                slope1[slot, x] = slope
+                slope1[i, slot, x] = slope
                 low = val.astype(bf16)
-                lifted[slot, x] = low
+                lifted[i, slot, x] = low
                 wide = low.astype(f32)
                 inv = lax.rsqrt(jnp.mean(wide * wide, axis=1, keepdims=True) + 1e-06)
                 normed = (wide * inv * gain_row).astype(bf16).astype(f32)
@@ -336,7 +351,7 @@
             loss = dwo = jnp.zeros((1, 128), f32)
             for x in range(8):
                 mixed, slope = gelu_both(pre2[x, slot])
-                hid = (lifted[slot, x].astype(f32) + mixed).astype(bf16).astype(f32)
+                hid = (lifted[i, slot, x].astype(f32) + mixed).astype(bf16).astype(f32)
                 pred = jnp.sum(hid * wo_row, axis=1, keepdims=True)
                 row = jnp.sum(jnp.where(sub8 == x, target, 0.0), axis=0, keepdims=True)
                 wanted = jnp.broadcast_to(row, (128, 128)).T
@@ -344,16 +359,16 @@
                 loss = loss + jnp.sum(misfit * misfit, axis=0, keepdims=True)
                 dwo = dwo + jnp.sum(hid * misfit, axis=0, keepdims=True)
                 d_hid = (misfit * wo_row).astype(bf16)
-                dh[slot, x] = d_hid
+                dh[i, slot, x] = d_hid
                 g = (d_hid.astype(f32) * slope).astype(bf16).astype(f32)
                 up, down = z_shifted(g, z_ids)
                 for k, v in enumerate((up, g, down)):
-                    gp[x + 1, slot, 1:5, :, k * 128 : (k + 1) * 128] = v.astype(bf16).reshape(4, 32, 128)
+                    gp[i, x + 1, slot, 1:5, :, k * 128 : (k + 1) * 128] = v.astype(bf16).reshape(4, 32, 128)
             lhs = jnp.concatenate(
                 [jnp.concatenate([nt[slot, q + x] for x in range(8)], axis=1) for q in range(3)], axis=0
             )
             for r in range(3):
-                rhs = gp[1:9, slot, 2 - r : 6 - r].reshape(1024, 384)
+                rhs = gp[i, 1:9, slot, 2 - r : 6 - r].reshape(1024, 384)
                 d = jnp.dot(lhs, rhs, preferred_element_type=f32)
                 for q in range(3):
                     for p in range(3):
@@ -363,27 +378,7 @@
             small[28:29, :] += dwo.astype(bf16).astype(f32)
             small[32:33, :] += 0.5 * loss
 
-    def second_part():
-        for x in range(8):
-            pre2[x] = conv_rows(gp, wb, x, -1)
-        for slot in range(PAIR):
-            dgain, dwl = jnp.zeros((1, 128), f32), jnp.zeros((32, 128), f32)
-            for x in range(8):
-                dn = pre2[x, slot].astype(bf16).astype(f32)
-                wide = lifted[slot, x].astype(f32)
-                inv = lax.rsqrt(jnp.mean(wide * wide, axis=1, keepdims=True) + 1e-06)
-                unit = wide * inv
-                dgain = dgain + jnp.sum(dn * unit, axis=0, keepdims=True)
-                dt = dn * gain_row
-                mean = jnp.sum(dt * wide, axis=1, keepdims=True) * (1.0 / 128.0)
-                d_low = dh[slot, x].astype(f32) + dt * inv - (inv * inv * inv * mean) * wide
-                d_pre = d_low.astype(bf16).astype(f32) * slope1[slot, x]
-                dwl = dwl + jnp.dot(nu[slot, x].astype(bf16), d_pre.astype(bf16), preferred_element_type=f32)
-            small[0:32, :] += dwl.astype(bf16).astype(f32)
-            small[27:28, :] += dgain
-
     def one_pair(i, carry):
-        pl.when(i > 0)(second_part)
         first_part(i)
         return carry
 
@@ -430,21 +425,48 @@
         started.append(copy)
         return copy
 
+    line_copies = []
+
+    def backward_steps():
+        dgain = jnp.zeros((1, 128), f32)
+        for pair in range(CAP // PAIR):
+            dwl = [jnp.zeros((32, 128), f32)] * PAIR
+            for x in range(8):
+                both = conv_rows(gp.at[pair], wb, x, -1)
+                for slot in range(PAIR):
+                    dn = both[slot].astype(bf16).astype(f32)
+                    wide = lifted[pair, slot, x].astype(f32)
+                    inv = lax.rsqrt(jnp.mean(wide * wide, axis=1, keepdims=True) + 1e-06)
+                    dgain = dgain + jnp.sum(dn * (wide * inv), axis=0, keepdims=True)
+                    dt = dn * gain_row
+                    mean = jnp.sum(dt * wide, axis=1, keepdims=True) * (1.0 / 128.0)
+                    d_low = dh[pair, slot, x].astype(f32) + dt * inv - (inv * inv * inv * mean) * wide
+                    d_pre = d_low.astype(bf16).astype(f32) * slope1[pair, slot, x]
+                    dwl[slot] = dwl[slot] + jnp.dot(
+                        nu[pair, slot, x].astype(bf16), d_pre.astype(bf16), preferred_element_type=f32
+                    )
+                yield
+            for part in dwl:
+                small[0:32, :] += part.astype(bf16).astype(f32)
+        small[27:28, :] += dgain
+        for k in range(n_gx):
+            pieces[k] = jnp.concatenate(
+                [small[per * k : per * k + per, :], jnp.zeros((8 - per, 128), f32)], axis=0
+            )
+        from_line_sums[gx] = pieces[gx]
+
+        line_copies.extend(
+            begin(remote(
+                pieces.at[device["gx"]], from_line_sums.at[gx], a_send.at[far], a_recv.at[far], device
+            ))
+            for far, device in line_partners(n_gx)
+        )
+        yield
+
     flying = {key: begin(ring_copy(0, *key)) for key in keys}
-    second_part()
-
-    for k in range(n_gx):
-        pieces[k] = jnp.concatenate(
-            [small[per * k : per * k + per, :], jnp.zeros((8 - per, 128), f32)], axis=0
-        )
-    from_line_sums[gx] = pieces[gx]
-
-    line_copies = [
-        begin(remote(
-            pieces.at[device["gx"]], from_line_sums.at[gx], a_send.at[far], a_recv.at[far], device
-        ))
-        for far, device in line_partners(n_gx)
-    ]
+    backward = backward_steps()
+    for _ in range(BEFORE):
+        next(backward)
 
     pairs = {}
     for step in range(far_side):
@@ -470,6 +492,7 @@
                     own.at[here], other.at[here], pair_send.at[part], pair_recv.at[part],
                     {"ga": 1 - ga},
                 ))
+            next(backward, None)
 
     for copy in line_copies:
         copy.wait_recv()
@@ -505,9 +528,11 @@
         copy.wait_recv()
 
     def emit(z, value):
-        new_field[z] = value
+        prev[z] = value
 
     advance(1, later, emit, False)
+    leave = [pltpu.make_async_copy(prev, new_field, load_sem.at[0])]
+    leave[0].start()
     for step in range(far_side):
         for key in keys:
             if step >= depth[key]:
@@ -528,7 +553,8 @@
                 for far, device in line_partners(n_gx)
             ]
 
-    total_out[...] = gathered[...]
+    leave.append(pltpu.make_async_copy(gathered, total_out, load_sem.at[1]))
+    leave[1].start()
     for copy in last_copies:
         copy.wait_recv()
     shared = jnp.concatenate([from_all[k, 0:per, :] for k in range(n_gx)], axis=0)
@@ -542,6 +568,8 @@
     tail_out[0:32, :] = shared * scale
     loss = small[32:33, :] / (PVOX * jnp.maximum(rank[0:1], 1.0))
     tail_out[32:40, :] = jnp.where(sub8 == 0, jnp.broadcast_to(scale, (8, 128)), loss)
+    for copy in leave:
+        copy.wait()
     for copy in started + first + halos + more:
         copy.wait_send()
 
@@ -555,7 +583,6 @@
     share = n_gy * n_ga
     rows = w_conv.shape[0] // n_gy
     far_side = n_gy // 2
-    smem = pl.BlockSpec(memory_space=pltpu.SMEM)
     vmem = pl.BlockSpec(memory_space=pltpu.VMEM)
     hbm = pl.BlockSpec(memory_space=pl.ANY)
     dma = pltpu.SemaphoreType.DMA
@@ -567,8 +594,8 @@
             jax.ShapeDtypeStruct((n_gy, rows, 128), bf16),
             jax.ShapeDtypeStruct((40, 128), f32),
         ),
-        in_specs=[smem] * 4 + [hbm] * 4 + [vmem, vmem, hbm, vmem],
-        out_specs=(vmem,) * 3,
+        in_specs=[hbm] * 8 + [vmem, vmem, hbm, vmem],
+        out_specs=(hbm, hbm, vmem),
         scratch_shapes=[
             held((size_z + 2, size_x, size_y), f32),
             held((size_z + 2, size_x, size_y), f32),
@@ -588,13 +615,13 @@
             held((3, 384, 384), bf16),
             held((32, 128), f32),
             held((10, PAIR, 6, 32, 384), bf16),
-            held((10, PAIR, 6, 32, 384), bf16),
+            held((CAP // PAIR, 10, PAIR, 6, 32, 384), bf16),
             held((PAIR, 10, 128, 128), bf16),
-            held((PAIR, 8, 32, 128), f32),
-            held((PAIR, 8, 128, 128), bf16),
-            held((PAIR, 8, 128, 128), f32),
+            held((CAP // PAIR, PAIR, 8, 32, 128), f32),
+            held((CAP // PAIR, PAIR, 8, 128, 128), bf16),
+            held((CAP // PAIR, PAIR, 8, 128, 128), f32),
             held((8, PAIR, 128, 128), f32),
-            held((PAIR, 8, 128, 128), bf16),
+            held((CAP // PAIR, PAIR, 8, 128, 128), bf16),
             held(w_conv.shape, f32),
             held((40, 128), f32),
             held((2, rows, 128), bf16),
@@ -609,7 +636,7 @@
             held((share, 8, 128), f32),
             held((8, 128), f32),
             held((n_gx, 8, 128), f32),
-            dma((5,)),
+            dma((9,)),
             dma((n_gx,)), dma((n_gx,)),
             dma((STEPS * 5,)), dma((STEPS * 5,)),
             dma((far_side, 2, 4)), dma((far_side, 2, 4)),
@@ -618,6 +645,10 @@
             dma((n_gx,)), dma((n_gx,)),
             dma((share,)), dma((share,)),
             dma((n_gx,)), dma((n_gx,)),
+            pltpu.SMEM((1,), jnp.int32),
+            pltpu.SMEM((2,), jnp.int32),
+            pltpu.SMEM((2,), jnp.int32),
+            pltpu.SMEM((2,), jnp.int32),
         ],
         compiler_params=pltpu.CompilerParams(
             collective_id=0, has_side_effects=True, vmem_limit_bytes=56 * 1024 * 1024

time: 79.5 us -> 75.7 us (0.952)
  Pallas kernels: 78.1 us -> 74.2 us
    pallas_call x1, Pallas kernels: 75.3 us -> 71.4 us  [whole_call(): pl.pallas_call(functools.partial(whole_kernel, n_gx, n_gy, n_ga, rows, en...]
where the time goes in v5:
time: 75.7 us; the launch traced here: 75.5 us
  Pallas kernels  74.2 us (98%)
  between operations  1.29 us (2%)
    pallas_call x1, Pallas kernels, whole_call(): pl.pallas_call(functools.partial(whole_kernel, n_gx, n_gy, n_ga, rows, en...  71.4 us
    pallas_call x1, Pallas kernels, finish_call(): pl.pallas_call(finish_kernel, out_shape=(tile((total.shape[0] * total.sha...  2.8 us

profile of v5, /device:TPU:1, one launch (start us, length us, event | category | flops | bytes accessed | tf_op | source)
XLA Modules:
  0.0 75.5 jit_solution(14956550109116567436)
XLA Ops:
  1.3 71.4 %shard_map.163 = (f32[32,32,128]{2,1,0:T(8,128)}, bf16[8,432,128]{2,1,0:T(8,128)(2,1)}, f32[40,128]{1,0:T(8,128)}) custom-call(s32[1]{0:T(128)} %bitcast.12.count_in, s32[2]{0:T(128)} %bitcast.14, s32[2]{0:T(128)} %bitcast.15, s32[2]{0:T(128)} %bitcast.16, f32[32,32,128]{2,1,0:T(8,128)} %field.1, f32[32,32,128]{2,1,0:T(8,128)} %prev_field.1, ...), custom_call_target="tpu_custom_call" | custom-call | tf_op jit(solution)/shard_map/pallas_call | solution.py:590
  72.7 2.8 %shard_map.164 = (f32[3456,128]{1,0:T(8,128)}, f32[27,128]{1,0:T(8,128)}, f32[1,128]{1,0:T(1,128)}, f32[1,128]{1,0:T(1,128)}, f32[1,128]{1,0:T(1,128)}, /*index=5*/f32[32,32,128]{2,1,0:T(8,128)}) custom-call(bf16[8,432,128]{2,1,0:T(8,128)(2,1)} %get-tuple-element.15.total, f32[40,128]{1,0:T(8,128)} %get-tuple-element.16.tail, ...), custom_call_target="tpu_custom_call" | custom-call | tf_op jit(solution)/shard_map/pallas_call | solution.py:677

commit v6 on v5

--- a/solution.py
+++ b/solution.py
@@ -215,13 +215,11 @@
             store(z, result)
             return place(z, result, *faces) if pack else faces
 
+        if not pack:
+            return layer
         return several(size_z, layer, (zero_tile, zero_tile))
 
     loads[0].wait()
-    high, low = several(
-        size_z, lambda z, faces: place(z, state[z + 1], *faces), (zero_tile, zero_tile)
-    )
-    pack_faces(0, state, high, low)
     loads[1].wait()
     for load in loads[5:]:
         load.wait()
@@ -250,6 +248,10 @@
         copy = remote(mine, line.at[gx], line_send.at[far], line_recv.at[far], device)
         copy.start()
         first.append(copy)
+    high, low = several(
+        size_z, lambda z, faces: place(z, state[z + 1], *faces), (zero_tile, zero_tile)
+    )
+    pack_faces(0, state, high, low)
     halos = halo_copies(0, state)
     for copy in halos:
         copy.start()
@@ -426,6 +428,10 @@
         return copy
 
     line_copies = []
+    leave = [pltpu.make_async_copy(prev, new_field, load_sem.at[0])]
+
+    def emit(z, value):
+        prev[z] = value
 
     def backward_steps():
         dgain = jnp.zeros((1, 128), f32)
@@ -462,6 +468,14 @@
             for far, device in line_partners(n_gx)
         )
         yield
+        for copy in more:
+            copy.wait_recv()
+        layer = advance(1, later, emit, False)
+        for z in range(size_z):
+            layer(z, None)
+            if z % 4 == 3:
+                yield
+        leave[0].start()
 
     flying = {key: begin(ring_copy(0, *key)) for key in keys}
     backward = backward_steps()
@@ -493,6 +507,8 @@
                     {"ga": 1 - ga},
                 ))
             next(backward, None)
+    for _ in backward:
+        pass
 
     for copy in line_copies:
         copy.wait_recv()
@@ -524,15 +540,6 @@
         for far, device in group_partners(n_gy, n_ga)
     ]
 
-    for copy in more:
-        copy.wait_recv()
-
-    def emit(z, value):
-        prev[z] = value
-
-    advance(1, later, emit, False)
-    leave = [pltpu.make_async_copy(prev, new_field, load_sem.at[0])]
-    leave[0].start()
     for step in range(far_side):
         for key in keys:
             if step >= depth[key]:

time: 75.7 us -> 75.8 us (level)
  no operation moved by 1% of the time
where the time goes in v6:
time: 75.8 us; the launch traced here: 75.6 us
  Pallas kernels  74.3 us (98%)
  between operations  1.29 us (2%)
    pallas_call x1, Pallas kernels, whole_call(): pl.pallas_call(functools.partial(whole_kernel, n_gx, n_gy, n_ga, rows, en...  71.5 us
    pallas_call x1, Pallas kernels, finish_call(): pl.pallas_call(finish_kernel, out_shape=(tile((total.shape[0] * total.sha...  2.8 us

profile of v6, /device:TPU:1, one launch (start us, length us, event | category | flops | bytes accessed | tf_op | source)
XLA Modules:
  0.0 75.6 jit_solution(1966743462769092191)
XLA Ops:
  1.3 71.5 %shard_map.163 = (f32[32,32,128]{2,1,0:T(8,128)}, bf16[8,432,128]{2,1,0:T(8,128)(2,1)}, f32[40,128]{1,0:T(8,128)}) custom-call(s32[1]{0:T(128)} %bitcast.12.count_in, s32[2]{0:T(128)} %bitcast.14, s32[2]{0:T(128)} %bitcast.15, s32[2]{0:T(128)} %bitcast.16, f32[32,32,128]{2,1,0:T(8,128)} %field.1, f32[32,32,128]{2,1,0:T(8,128)} %prev_field.1, ...), custom_call_target="tpu_custom_call" | custom-call | tf_op jit(solution)/shard_map/pallas_call | solution.py:597
  72.8 2.8 %shard_map.164 = (f32[3456,128]{1,0:T(8,128)}, f32[27,128]{1,0:T(8,128)}, f32[1,128]{1,0:T(1,128)}, f32[1,128]{1,0:T(1,128)}, f32[1,128]{1,0:T(1,128)}, /*index=5*/f32[32,32,128]{2,1,0:T(8,128)}) custom-call(bf16[8,432,128]{2,1,0:T(8,128)(2,1)} %get-tuple-element.15.total, f32[40,128]{1,0:T(8,128)} %get-tuple-element.16.tail, ...), custom_call_target="tpu_custom_call" | custom-call | tf_op jit(solution)/shard_map/pallas_call | solution.py:684
